TPU v7x, 256 devices: a whole 4x4x8 slice. The times are simulated.
256 devices in a mesh: section: 16 (over x, z_lo, core), seq: 16 (over y, z_hi).
Axes of the slice: x: 4, y: 4, z: 8 (z_hi: 4, z_lo: 2; z = z_hi * 2 + z_lo), core: 2. Of those that a mesh axis runs over, the one named last changes fastest.
Arguments:
- embed_table: bfloat16 [131072, 5376], P(('section', 'seq')), may hold values from -72 to 72
- vocab_shard: int32 [2048, 1], P('seq'), may hold values from 0 to 255; in each aligned block of 128 rows (0 to 127, 128 to 255, ...) at most 2 rows name the same one
- shard_row: int32 [2048], P('seq'), may hold values from 0 to 511
- norm_gain: bfloat16 [5376], replicated, may hold values from 0.099609375 to 1.8984375
- weight: bfloat16 [5376, 8192], P('seq', 'section'), may hold values from -0.078125 to 0.078125
- cotangent: bfloat16 [2048, 8192], P('seq', 'section'), may hold values from -6 to 6
Outputs:
- projected: bfloat16 [2048, 8192], P('seq', 'section')
- table_grad: bfloat16 [131072, 5376], P(('section', 'seq'))
- weight_grad: bfloat16 [5376, 8192], P('seq', 'section')
Inputs may be any that keep to these rules, and one draw needn't show every extreme that they name: `vocab_shard`: in each aligned block of 128 tokens no shard is named by more than 2 tokens, a bound that some block reaches.
All inputs are finite; a program needn't handle non-finite values.
Results may differ from a plain program's by a relative error of at most 0.024.
Values may be sent and summed in bfloat16 or wider, within the bound.
No kernel may reach another device: no remote copies, remote signals or barrier semaphores. Data moves between devices by JAX's collectives and lax.ppermute only.
A program may use at most 128 MiB of HBM per device.

v0:
```python
import jax
import jax.numpy as jnp
from jax import lax
from jax.sharding import PartitionSpec as P

EPS = 1e-06


def look_up(embed_table, wanted):
    found = jnp.take(embed_table, jnp.maximum(wanted, 0), axis=0)
    return jnp.where((wanted >= 0)[..., None], found, jnp.zeros((), embed_table.dtype))


def to_tokens(answer_rows, slot_index, model_width):
    padded = jnp.concatenate(
        [answer_rows.reshape(-1, model_width), jnp.zeros((1, model_width), answer_rows.dtype)],
        axis=0,
    )
    return jnp.take(padded, slot_index, axis=0)


def slot_ranks(target, column_count, active):
    dest_hits = jnp.logical_and(
        target[:, None] == jnp.arange(column_count, dtype=jnp.int32)[None, :], active[:, None]
    )
    counts = jnp.cumsum(dest_hits.astype(jnp.int32), axis=0) - 1
    return jnp.sum(jnp.where(dest_hits, counts, 0), axis=1)


def norm_back(upstream, unit_rows, inv_rms, gain_full):
    scaled = upstream * gain_full
    return inv_rms * (scaled - unit_rows * jnp.mean(scaled * unit_rows, axis=-1, keepdims=True))


def per_device(embed_table, vocab_shard, shard_row, norm_gain, weight, cotangent):
    n_section = lax.axis_size("section")
    n_seq = lax.axis_size("seq")
    tok_rows = shard_row.shape[0]
    vocab_rows = embed_table.shape[0]
    model_width = embed_table.shape[1]
    capacity = max(2, 3 * tok_rows // (n_section * n_seq))
    owner_shard = vocab_shard[:, 0]
    is_mine = owner_shard // n_seq == lax.axis_index("section")
    dest_seq = owner_shard % n_seq
    slot_rank = slot_ranks(dest_seq, n_seq, is_mine)
    slot_index = jnp.where(is_mine, dest_seq * capacity + slot_rank, n_seq * capacity)
    requests = (
        jnp.full((n_seq * capacity + 1,), -1, jnp.int32)
        .at[slot_index]
        .set(shard_row)[:-1]
        .reshape(n_seq, capacity)
    )
    asked_rows = lax.all_to_all(requests, "seq", split_axis=0, concat_axis=0, tiled=True)
    answer = lax.all_to_all(
        look_up(embed_table, asked_rows), "seq", split_axis=0, concat_axis=0, tiled=True
    )
    section_rows = to_tokens(answer, slot_index, model_width).astype(jnp.float32)
    embedded = lax.psum(section_rows.astype(jnp.bfloat16), "section").astype(jnp.float32)
    inv_rms = lax.rsqrt(jnp.mean(embedded * embedded, axis=-1, keepdims=True) + EPS)
    unit_rows = embedded * inv_rms
    gain_full = norm_gain.astype(jnp.float32)
    normed = (unit_rows * gain_full).astype(jnp.bfloat16)
    w_full = lax.all_gather(weight, "seq", axis=0, tiled=True)
    projected = jnp.dot(normed, w_full, preferred_element_type=jnp.float32).astype(jnp.bfloat16)
    upstream_part = lax.dot_general(
        cotangent, w_full, (((1,), (1,)), ((), ())), preferred_element_type=jnp.float32
    )
    share_rows = tok_rows // n_section
    first_row = lax.axis_index("section") * share_rows
    upstream_share = lax.psum_scatter(
        upstream_part.astype(jnp.bfloat16), "section", scatter_dimension=0, tiled=True
    ).astype(jnp.float32)
    unit_share = lax.dynamic_slice_in_dim(unit_rows, first_row, share_rows, 0)
    rms_share = lax.dynamic_slice_in_dim(inv_rms, first_row, share_rows, 0)
    grad_share = norm_back(upstream_share, unit_share, rms_share, gain_full).astype(jnp.bfloat16)
    row_grads = lax.all_gather(grad_share, "section", axis=0, tiled=True)
    grad_buffer = (
        jnp.zeros((n_seq * capacity + 1, model_width), jnp.bfloat16)
        .at[slot_index]
        .set(row_grads)[:-1]
    )
    grad_buffer = grad_buffer.reshape(n_seq, capacity, model_width)
    got_grads, got_rows = (
        lax.all_to_all(grad_buffer, "seq", split_axis=0, concat_axis=0, tiled=True),
        lax.all_to_all(requests, "seq", split_axis=0, concat_axis=0, tiled=True),
    )
    pick_matrix = (
        jnp.arange(vocab_rows, dtype=jnp.int32)[:, None] == got_rows.reshape(1, -1)
    ).astype(jnp.bfloat16)
    table_grad = jnp.dot(
        pick_matrix, got_grads.reshape(-1, model_width), preferred_element_type=jnp.float32
    ).astype(jnp.bfloat16)
    weight_grad = lax.psum_scatter(
        lax.dot_general(
            normed, cotangent, (((0,), (0,)), ((), ())), preferred_element_type=jnp.float32
        ).astype(jnp.bfloat16),
        "seq",
        scatter_dimension=0,
        tiled=True,
    )
    return (projected, table_grad, weight_grad)


def solution(mesh):
    in_specs = (
        P(("section", "seq"), None),
        P("seq", None),
        P("seq"),
        P(),
        P("seq", "section"),
        P("seq", "section"),
    )
    out_specs = (P("seq", "section"), P(("section", "seq"), None), P("seq", "section"))
    return jax.shard_map(
        per_device, mesh=mesh, in_specs=in_specs, out_specs=out_specs, check_vma=False
    )
```

profile of v0, /device:TPU:8, one launch (start us, length us, event | category | flops | bytes accessed | tf_op | source)
XLA Modules:
  0.0 400.5 jit_solution(15420816363327021555)
XLA Ops:
  8.0 0.0 all-gather.3.cloned.1.call-start
  8.1 0.7 all-gather.3.cloned.1.call-update
  8.8 0.7 compare_bitcast_fusion.2
  9.4 0.1 fusion.5
  9.5 0.2 reduce_window_sum.11
  9.7 0.2 select_reduce_fusion
  9.9 1.1 scatter_custom_fusion
  11.0 0.1 all_to_all.13
  11.1 20.0 %all_to_all.20 = s32[16,1,2]{2,1,0:T(1,128)S(1)} all-to-all(s32[16,1,2]{2,1,0:T(1,128)S(1)} %bitcast.27), channel_id=1, replica_groups=mesh['section'=16,'seq'=16] {'seq'}, dimensions={0} | all-to-all | bytes 256 | tf_op jit(solution)/shard_map/all_to_all | solution.py:53
  31.1 0.1 copy.23
  31.1 0.1 copy.26
  31.2 0.1 copy.24
  31.3 0.1 copy.27
  31.4 0.1 reshape.90
  31.5 4.4 %gather_fusion = bf16[32,5376]{1,0:T(8,128)(2,1)S(1)} fusion(bf16[512,5376]{1,0:T(8,128)(2,1)} %param.6, s32[1024]{0:T(1024)S(1)} %pad_clamp_fusion.1), kind=kCustom, calls=%fused_computation | custom fusion | bytes 688256 | tf_op jit(solution)/shard_map/jit(_take)/gather | solution.py:10
  35.9 0.1 reshape.89
  36.0 1.3 broadcast_select_fusion.2
  37.3 4.8 %all-to-all-start.1 = ((bf16[16,2,5376]{2,1,0:T(2,128)(2,1)}), bf16[16,2,5376]{2,1,0:T(2,128)(2,1)S(1)}, u32[]{:S(2)}, u32[]{:S(2)}) async-start(bf16[16,2,5376]{2,1,0:T(2,128)(2,1)} %broadcast_select_fusion.2), calls=%async_computation.1 | async-start | bytes 688128 | tf_op jit(solution)/shard_map/all_to_all | solution.py:54
  42.1 0.0 all-reduce.3.cloned.1.call-start
  42.2 11.3 %all-to-all-done.1 = bf16[16,2,5376]{2,1,0:T(2,128)(2,1)S(1)} async-done(((bf16[16,2,5376]{2,1,0:T(2,128)(2,1)}), bf16[16,2,5376]{2,1,0:T(2,128)(2,1)S(1)}, u32[]{:S(2)}, u32[]{:S(2)}) %all-to-all-start.1) | async-done | bytes 344096 | tf_op jit(solution)/shard_map/all_to_all | solution.py:54
  53.5 0.1 reshape.85
  53.7 1.4 gather_fusion.1
  55.1 1.3 broadcast_select_fusion
  56.4 0.0 reduce-scatter.3.cloned.1.call-start
  56.5 52.5 %all-gather.3.cloned.1.call-done = bf16[5376,512]{1,0:T(8,128)(2,1)} async-done(((bf16[336,512]{1,0:T(8,128)(2,1)}), bf16[5376,512]{1,0:T(8,128)(2,1)}) %all-gather.3.cloned.1.call-update) | async-done | bytes 5505040 | tf_op jit(solution)/shard_map/all_gather | solution.py:63
  108.9 5.5 %convolution_convert_fusion.2 = bf16[128,5376]{1,0:T(8,128)(2,1)} fusion(bf16[128,512]{1,0:T(8,128)(2,1)S(1)} %copy-done, bf16[5376,512]{1,0:T(8,128)(2,1)} %all-gather.3.cloned.1.call-done), kind=kOutput, calls=%fused_computation.6 | convolution fusion | flops 705331200 | bytes 7012352 | tf_op jit(solution)/shard_map/dot_general | solution.py:65
  114.5 0.0 all-gather.5.cloned.1.call-start
  114.6 96.6 %all-reduce.3.cloned.1.call-done = bf16[128,5376]{1,0:T(8,128)(2,1)} async-done(((bf16[128,5376]{1,0:T(8,128)(2,1)}), bf16[128,5376]{1,0:T(8,128)(2,1)}) %all-reduce.3.cloned.1.call-update) | async-done | bytes 1376272 | tf_op jit(solution)/shard_map/psum | solution.py:58
  211.2 1.7 fusion
  212.9 0.1 dynamic-slice.3
  213.0 3.2 convert_multiply_fusion
  216.2 61.9 %reduce-scatter.3.cloned.1.call-done = bf16[8,5376]{1,0:T(8,128)(2,1)} async-done(((bf16[128,5376]{1,0:T(8,128)(2,1)}), bf16[8,5376]{1,0:T(8,128)(2,1)}) %reduce-scatter.3.cloned.1.call-update) | async-done | bytes 86032 | tf_op jit(solution)/shard_map/reduce_scatter | solution.py:70
  278.1 1.1 multiply_reduce_fusion
  279.3 1.7 multiply_convert_fusion.3
  281.0 0.0 reduce-scatter.5.cloned.1.call-start
  281.0 4.2 %convolution_convert_fusion = bf16[5376,512]{1,0:T(8,128)(2,1)} fusion(bf16[128,512]{1,0:T(8,128)(2,1)S(1)} %copy-done, f32[5376]{0:T(1024)S(1)} %convert_element_type.35, bf16[128,5376]{1,0:T(8,128)(2,1)S(1)} %copy-done.1, f32[128]{0:T(128)S(1)} %add_rsqrt_fusion), kind=kOutput, calls=%fused_computation.4 | convolution fusion | flops 710148096 | bytes 7034368 | tf_op jit(solution)/shard_map/dot_general | solution.py:94
  285.2 33.1 %all-gather.5.cloned.1.call-done = bf16[128,5376]{1,0:T(8,128)(2,1)} async-done(((bf16[8,5376]{1,0:T(8,128)(2,1)}), bf16[128,5376]{1,0:T(8,128)(2,1)}) %all-gather.5.cloned.1.call-update) | async-done | bytes 1376272 | tf_op jit(solution)/shard_map/all_gather | solution.py:76
  318.3 3.2 scatter_custom_fusion.1
  321.6 0.9 reshape.86
  322.4 12.6 %all-to-all-start.2 = ((bf16[16,2,5376]{2,1,0:T(2,128)(2,1)}), bf16[16,2,5376]{2,1,0:T(2,128)(2,1)S(1)}, u32[]{:S(2)}, u32[]{:S(2)}) async-start(bf16[16,2,5376]{2,1,0:T(2,128)(2,1)} %reshape.86), calls=%async_computation.3 | async-start | bytes 688128 | tf_op jit(solution)/shard_map/all_to_all | solution.py:84
  335.0 0.5 broadcast.170
  335.6 0.7 reduce.3
  336.2 0.1 eq.48
  336.3 4.2 %convolution_convert_fusion.3 = bf16[128,512]{1,0:T(8,128)(2,1)} fusion(bf16[5376,512]{1,0:T(8,128)(2,1)} %all-gather.3.cloned.1.call-done, f32[5376]{0:T(1024)S(1)} %convert_element_type.35, bf16[128,5376]{1,0:T(8,128)(2,1)S(1)} %copy-done.1, f32[128]{0:T(128)S(1)} %add_rsqrt_fusion), kind=kOutput, calls=%fused_computation.12 | convolution fusion | flops 707461120 | bytes 7034368 | tf_op jit(solution)/shard_map/dot_general | solution.py:64
  340.5 15.0 %all-to-all-done.2 = bf16[16,2,5376]{2,1,0:T(2,128)(2,1)S(1)} async-done(((bf16[16,2,5376]{2,1,0:T(2,128)(2,1)}), bf16[16,2,5376]{2,1,0:T(2,128)(2,1)S(1)}, u32[]{:S(2)}, u32[]{:S(2)}) %all-to-all-start.2) | async-done | bytes 344096 | tf_op jit(solution)/shard_map/all_to_all | solution.py:84
  355.5 0.1 reshape.87
  355.6 4.0 %convolution_convert_fusion.1 = bf16[512,5376]{1,0:T(8,128)(2,1)} fusion(bf16[32,5376]{1,0:T(8,128)(2,1)S(1)} %reshape.87, s32[32]{0:T(128)S(1)} %eq.48), kind=kOutput, calls=%fused_computation.5 | convolution fusion | flops 178929664 | bytes 5849216 | tf_op jit(solution)/shard_map/dot_general | solution.py:90
  359.7 33.3 %reduce-scatter.5.cloned.1.call-done = bf16[336,512]{1,0:T(8,128)(2,1)} async-done(((bf16[5376,512]{1,0:T(8,128)(2,1)}), bf16[336,512]{1,0:T(8,128)(2,1)}) %reduce-scatter.5.cloned.1.call-update) | async-done | bytes 344080 | tf_op jit(solution)/shard_map/reduce_scatter | solution.py:93
  (21 shorter events, 0.2 us)
Async XLA Ops:
  8.0 101.0 %copy-start = (bf16[128,512]{1,0:T(8,128)(2,1)S(1)}, bf16[128,512]{1,0:T(8,128)(2,1)}, u32[]{:S(2)}) copy-start(bf16[128,512]{1,0:T(8,128)(2,1)} %param.11) | copy-start | bytes 393220
  8.0 100.9 %all-gather.3.cloned.1.call-start = ((), (), s32[]{:S(2)}) async-start(), calls=%async_computation.6 | async-start | bytes 5849088 | tf_op jit(solution)/shard_map/all_gather | solution.py:63
  37.3 16.2 %all-to-all-start.1 = ((bf16[16,2,5376]{2,1,0:T(2,128)(2,1)}), bf16[16,2,5376]{2,1,0:T(2,128)(2,1)S(1)}, u32[]{:S(2)}, u32[]{:S(2)}) async-start(bf16[16,2,5376]{2,1,0:T(2,128)(2,1)} %broadcast_select_fusion.2), calls=%async_computation.1 | async-start | bytes 688128 | tf_op jit(solution)/shard_map/all_to_all | solution.py:54
  42.1 169.1 %all-reduce.3.cloned.1.call-start = ((), (), s32[]{:S(2)}) async-start(), calls=%async_computation.5 | async-start | bytes 2752512 | tf_op jit(solution)/shard_map/psum | solution.py:58
  56.4 58.2 %copy-start.2 = (bf16[5376]{0:T(1024)(128)(2,1)S(1)}, bf16[5376]{0:T(1024)(128)(2,1)}, u32[]{:S(2)}) copy-start(bf16[5376]{0:T(1024)(128)(2,1)} %param.9) | copy-start | bytes 32260
  56.4 221.7 %reduce-scatter.3.cloned.1.call-start = ((), (), s32[]{:S(2)}) async-start(), calls=%async_computation.7 | async-start | bytes 1462272 | tf_op jit(solution)/shard_map/reduce_scatter | solution.py:70
  114.5 203.8 %all-gather.5.cloned.1.call-start = ((), (), s32[]{:S(2)}) async-start(), calls=%async_computation.8 | async-start | bytes 1462272 | tf_op jit(solution)/shard_map/all_gather | solution.py:76
  212.9 68.2 %copy-start.1 = (bf16[128,5376]{1,0:T(8,128)(2,1)S(1)}, bf16[128,5376]{1,0:T(8,128)(2,1)}, u32[]{:S(2)}) copy-start(bf16[128,5376]{1,0:T(8,128)(2,1)} %all-reduce.3.cloned.1.call-done) | copy-start | bytes 4128772
  281.0 111.9 %reduce-scatter.5.cloned.1.call-start = ((), (), s32[]{:S(2)}) async-start(), calls=%async_computation.9 | async-start | bytes 5849088 | tf_op jit(solution)/shard_map/reduce_scatter | solution.py:93
  322.4 33.1 %all-to-all-start.2 = ((bf16[16,2,5376]{2,1,0:T(2,128)(2,1)}), bf16[16,2,5376]{2,1,0:T(2,128)(2,1)S(1)}, u32[]{:S(2)}, u32[]{:S(2)}) async-start(bf16[16,2,5376]{2,1,0:T(2,128)(2,1)} %reshape.86), calls=%async_computation.3 | async-start | bytes 688128 | tf_op jit(solution)/shard_map/all_to_all | solution.py:84
Sparse Core Ops, SparseCore 0:
  11.3 97.5 all-gather.2
  286.1 106.8 reduce-scatter.4
Sparse Core Ops, SparseCore 1:
  56.5 154.6 all-reduce.2
  213.6 64.5 reduce-scatter.2
  281.1 37.2 all-gather.4
where the time goes:
time: 402 us; the launch traced here: 400 us
  waiting for transfers between devices  304 us (76%)
  blocking collectives  20 us (5%)
  matrix products  17.9 us (4%)
  starting transfers between devices  17.7 us (4%)
  between operations  15.8 us (4%)
  local copies, waits for them, and re-layouts  12.6 us (3%)
  other arithmetic  12.1 us (3%)
    psum x1, waiting for transfers between devices, per_device(): lax.psum(section_rows.astype(jnp.bfloat16), 'section').astype(jnp.float32)  96.6 us
    reduce_scatter x1, waiting for transfers between devices, per_device(): lax.psum_scatter(upstream_part.astype(jnp.bfloat16), 'section', scatter_d...  61.9 us
    all_gather x1, waiting for transfers between devices, per_device(): w_full = lax.all_gather(weight, 'seq', axis=0, tiled=True)  52.5 us
    reduce_scatter x1, waiting for transfers between devices, per_device(): lax.psum_scatter(lax.dot_general(normed, cotangent, (((0,), (0,)), ((), (...  33.3 us
    all_gather x1, waiting for transfers between devices, per_device(): row_grads = lax.all_gather(grad_share, 'section', axis=0, tiled=True)  33.1 us
    all_to_all x1, blocking collectives, per_device(): lax.all_to_all(requests, 'seq', split_axis=0, concat_axis=0, tiled=True)  20 us
    all_to_all x1, waiting for transfers between devices, per_device(): lax.all_to_all(grad_buffer, 'seq', split_axis=0, concat_axis=0, tiled=True)  15 us
    all_to_all x1, starting transfers between devices, per_device(): lax.all_to_all(grad_buffer, 'seq', split_axis=0, concat_axis=0, tiled=True)  12.6 us
  transfers between devices with their start and end apart: 7, of which 7 were waited for; matrix products, arithmetic and copies ran while one was open for 10% of the time, Pallas kernels for 0%

commit v1 on v0

v1 whole, which is shorter than its diff:
```python
import jax
import jax.numpy as jnp
from jax import lax
from jax.sharding import Mesh, PartitionSpec as P

EPS = 1e-06
SECTION = ("x", "z_lo", "core")
SEQ = ("y", "z_hi")
CAP = 2
BF16 = jnp.bfloat16
F32 = jnp.float32


def dot(a, b, contract):
    return lax.dot_general(a, b, (contract, ((), ())), preferred_element_type=F32)


def swap_cores(x):
    return lax.ppermute(x, "core", [(0, 1), (1, 0)])


def exchange(x, axes):
    return lax.all_to_all(x, axes, split_axis=0, concat_axis=0, tiled=True)


def owner_rows(token_ids, shard, vocab_rows):
    tokens = token_ids.shape[1]
    mine = token_ids // vocab_rows == shard
    place = jnp.arange(tokens, dtype=jnp.int32)[None, :]
    first = jnp.min(jnp.where(mine, place, tokens), axis=1, keepdims=True)
    last = jnp.max(jnp.where(mine, place, -1), axis=1, keepdims=True)
    row = token_ids % vocab_rows
    row_first = jnp.sum(jnp.where(place == first, row, 0), axis=1)
    row_last = jnp.sum(jnp.where(place == last, row, 0), axis=1)
    some = last[:, 0] >= 0
    two = jnp.logical_and(some, last[:, 0] != first[:, 0])
    return jnp.stack([jnp.where(some, row_first, -1), jnp.where(two, row_last, -1)], axis=1)


def token_slots(block_ids, vocab_rows):
    shard = block_ids // vocab_rows
    place = jnp.arange(shard.shape[0], dtype=jnp.int32)
    earlier = jnp.logical_and(shard[:, None] == shard[None, :], place[None, :] < place[:, None])
    return shard * CAP + jnp.sum(earlier.astype(jnp.int32), axis=1)


def per_device(embed_table, vocab_shard, shard_row, norm_gain, weight, cotangent):
    nx, nzl, nc = (lax.axis_size(a) for a in SECTION)
    ny, nzh = (lax.axis_size(a) for a in SEQ)
    n_section, n_seq = nx * nzl * nc, ny * nzh
    vocab_rows, model_width = embed_table.shape
    tok = shard_row.shape[0]
    feat, cols = weight.shape
    section, seq = lax.axis_index(SECTION), lax.axis_index(SEQ)
    core, y = lax.axis_index("core"), lax.axis_index("y")
    section_x = lax.axis_index("x")
    nb, nf = nx, nzl * nc
    block_slots = n_seq * CAP
    slots = n_section * block_slots

    ids = vocab_shard[:, 0] * vocab_rows + shard_row
    all_ids = exchange(jnp.broadcast_to(ids[None], (n_seq, tok)), SEQ)

    w_y = lax.all_gather(weight, "y", axis=0)
    cot = lax.all_gather(cotangent, "z_hi", axis=0, tiled=True)
    w_y = w_y.reshape(nzl, nc, feat, cols)
    w_own = lax.dynamic_index_in_dim(w_y, core, 1, keepdims=False)
    w_other = lax.dynamic_index_in_dim(w_y, 1 - core, 1, keepdims=False)

    wanted = owner_rows(all_ids, section * n_seq + seq, vocab_rows).reshape(-1)
    found = jnp.take(embed_table, jnp.maximum(wanted, 0), axis=0)
    embedded = jnp.where((wanted >= 0)[:, None], found, jnp.zeros((), BF16)).astype(F32)
    inv_rms = lax.rsqrt(jnp.mean(embedded * embedded, axis=-1, keepdims=True) + EPS)
    unit_rows = embedded * inv_rms
    gain_full = norm_gain.astype(F32)
    normed_rows = (unit_rows * gain_full).astype(BF16)

    out_rows = normed_rows.reshape(ny, nb * CAP, nf, nzh, feat).transpose(0, 3, 2, 1, 4)
    got = exchange(out_rows.reshape(n_seq, nf * nb * CAP, feat), SEQ)
    got = got.reshape(n_seq, nf, nb, CAP, feat).transpose(2, 1, 0, 3, 4)
    got = exchange(got.reshape(n_section, block_slots, feat), SECTION)
    block_ids = lax.dynamic_index_in_dim(all_ids, y * nzh + section_x, 0, keepdims=False)
    slot = token_slots(block_ids, vocab_rows)
    place = (slot[:, None] == jnp.arange(slots, dtype=jnp.int32)[None, :]).astype(BF16)
    normed_block = dot(place, got.reshape(slots, feat), ((1,), (0,))).astype(BF16)

    n_own = lax.all_gather(normed_block, ("x", "z_lo"), axis=0).reshape(nb, nzl, tok, feat)
    n_other = swap_cores(n_own)

    def partial_up(w):
        return jnp.stack([dot(cot, w[k], ((1,), (1,))) for k in range(nzl)])
    up = partial_up(w_own) + swap_cores(partial_up(w_other).astype(BF16)).astype(F32)
    up = up.astype(BF16).reshape(nzl, nb, tok, feat).transpose(1, 0, 2, 3)
    up = exchange(up.reshape(nb * nzl, tok, feat), ("x", "z_lo"))
    up = jnp.sum(up.astype(F32), axis=0).astype(BF16)
    back = dot(place, up, ((0,), (0,))).astype(BF16).reshape(n_section, block_slots, feat)
    back = exchange(back, SECTION).reshape(nb, nf, n_seq, CAP, feat).transpose(2, 1, 0, 3, 4)
    back = exchange(back.reshape(n_seq, nf * nb * CAP, feat), SEQ)
    back = back.reshape(ny, nzh, nf, nb * CAP, feat).transpose(0, 3, 2, 1, 4)
    upstream = back.reshape(n_seq * CAP, model_width).astype(F32)
    scaled = upstream * gain_full
    row_grads = (
        inv_rms * (scaled - unit_rows * jnp.mean(scaled * unit_rows, axis=-1, keepdims=True))
    ).astype(BF16)
    pick = (jnp.arange(vocab_rows, dtype=jnp.int32)[:, None] == wanted[None, :]).astype(BF16)
    table_grad = dot(pick, row_grads, ((1,), (0,))).astype(BF16)

    def tokens_of(n, k):
        return n[:, k].reshape(nb * tok, feat)
    proj = sum(
        dot(tokens_of(n, k), w[k], ((1,), (0,)))
        for n, w in ((n_own, w_own), (n_other, w_other)) for k in range(nzl)
    )
    proj = exchange(proj.astype(BF16).reshape(nzh, tok, cols), "z_hi")
    projected = jnp.sum(proj.astype(F32), axis=0).astype(BF16)

    g_own = jnp.stack([dot(tokens_of(n_own, k), cot, ((0,), (0,))).astype(BF16) for k in range(nzl)])
    g_other = jnp.stack([dot(tokens_of(n_other, k), cot, ((0,), (0,))).astype(BF16) for k in range(nzl)])
    first, second = jnp.where(core == 0, g_own, g_other), jnp.where(core == 0, g_other, g_own)
    grad = jnp.stack([first, second], axis=1).reshape(ny, feat, cols)
    grad = exchange(grad, "y")
    weight_grad = jnp.sum(grad.astype(F32), axis=0).astype(BF16)
    return projected, table_grad, weight_grad


def solution(mesh):
    devices = mesh.devices.reshape(4, 2, 2, 4, 4)
    fine = Mesh(devices, SECTION + SEQ)
    in_specs = (
        P(SECTION + SEQ, None),
        P(SEQ, None),
        P(SEQ),
        P(),
        P(SEQ, SECTION),
        P(SEQ, SECTION),
    )
    out_specs = (P(SEQ, SECTION), P(SECTION + SEQ, None), P(SEQ, SECTION))
    return jax.shard_map(
        per_device, mesh=fine, in_specs=in_specs, out_specs=out_specs, check_vma=False
    )
```

time: 402 us -> 231 us (0.57)
  waiting for transfers between devices: 304 us -> 76.3 us
  blocking collectives: 20 us -> 64.9 us
  starting transfers between devices: 17.7 us -> 37.3 us
  other arithmetic: 12.1 us -> 5.62 us
    psum x1 -> x0, waiting for transfers between devices: 96.6 us -> none  [per_device(): lax.psum(section_rows.astype(jnp.bfloat16), 'section').astype(jnp.float32)]
    reduce_scatter x2 -> x0, waiting for transfers between devices: 95.2 us -> none  [the longest x1 61.9 us: per_device(): lax.psum_scatter(upstream_part.astype(jnp.bfloat16), 'section', scatter_d...]
    all_gather x2 -> x1, waiting for transfers between devices: 85.5 us -> 11.4 us  [per_device(): w_y = lax.all_gather(weight, 'y', axis=0)]
    all_gather x0 -> x2, blocking collectives: none -> 47.9 us  [the longest x1 27.6 us: per_device(): lax.all_gather(normed_block, ('x', 'z_lo'), axis=0)]
    all_to_all x2 -> x7, waiting for transfers between devices: 26.4 us -> 63.5 us  [exchange(): return lax.all_to_all(x, axes, split_axis=0, concat_axis=0, tiled=True)]
    all_to_all x2 -> x7, starting transfers between devices: 17.5 us -> 37.1 us  [exchange(): return lax.all_to_all(x, axes, split_axis=0, concat_axis=0, tiled=True)]
    scatter x2 -> x0, local copies, waits for them, and re-layouts: 4.33 us -> none  [the longest x1 3.23 us: per_device(): grad_buffer = jnp.zeros((n_seq * capacity + 1, model_width), jnp.bfloat16...]
    reshape x3 -> x8, local copies, waits for them, and re-layouts: 1.12 us -> 5.23 us  [the longest x2 2.61 us: per_device(): lax.all_gather(normed_block, ('x', 'z_lo'), axis=0)]
  transfers between devices with their start and end apart: 7 -> 10, of which waited for: 7 -> 9; matrix products, arithmetic and copies ran while one was open for 10% -> 10% of each run, Pallas kernels for 0% -> 0%
where the time goes in v1:
time: 231 us; the launch traced here: 229 us
  waiting for transfers between devices  76.3 us (33%)
  blocking collectives  64.9 us (28%)
  starting transfers between devices  37.3 us (16%)
  local copies, waits for them, and re-layouts  16.1 us (7%)
  matrix products  14.4 us (6%)
  between operations  14.4 us (6%)
  other arithmetic  5.62 us (2%)
    all_to_all x7, waiting for transfers between devices, exchange(): return lax.all_to_all(x, axes, split_axis=0, concat_axis=0, tiled=True)  63.5 us
    all_to_all x7, starting transfers between devices, exchange(): return lax.all_to_all(x, axes, split_axis=0, concat_axis=0, tiled=True)  37.1 us
    all_gather x1, blocking collectives, per_device(): lax.all_gather(normed_block, ('x', 'z_lo'), axis=0)  27.6 us
    all_gather x1, blocking collectives, per_device(): cot = lax.all_gather(cotangent, 'z_hi', axis=0, tiled=True)  20.3 us
    all_to_all x1, blocking collectives, exchange(): return lax.all_to_all(x, axes, split_axis=0, concat_axis=0, tiled=True)  17 us
    dot_general x15, matrix products, dot(): lax.dot_general(a, b, (contract, ((), ())), preferred_element_type=F32)  14.4 us
    all_gather x1, waiting for transfers between devices, per_device(): w_y = lax.all_gather(weight, 'y', axis=0)  11.4 us
    gather x2, local copies, waits for them, and re-layouts, per_device(): found = jnp.take(embed_table, jnp.maximum(wanted, 0), axis=0)  5.12 us
  transfers between devices with their start and end apart: 10, of which 9 were waited for; matrix products, arithmetic and copies ran while one was open for 10% of the time, Pallas kernels for 0%

profile of v1, /device:TPU:8, one launch (start us, length us, event | category | flops | bytes accessed | tf_op | source)
XLA Modules:
  0.0 229.1 jit_solution(2317120085725322106)
XLA Ops:
  7.2 0.7 all-gather.4.cloned.1.call-update
  7.9 20.3 %all_gather.19 = bf16[512,512]{1,0:T(8,128)(2,1)S(1)} all-gather(bf16[128,512]{1,0:T(8,128)(2,1)} %param.11), channel_id=1, replica_groups=mesh['x'=4,'z_lo'=2,'core'=2,'y'=4,'z_hi'=4] {'z_hi'}, dimensions={0}, use_global_device_ids=true | all-gather | bytes 655360 | tf_op jit(solution)/shard_map/all_gather | solution.py:65
  28.2 11.4 %all-gather.4.cloned.1.call-done = bf16[1344,512]{1,0:T(8,128)(2,1)} async-done(((bf16[336,512]{1,0:T(8,128)(2,1)}), bf16[1344,512]{1,0:T(8,128)(2,1)}) %all-gather.4.cloned.1.call-update) | async-done | bytes 1376272 | tf_op jit(solution)/shard_map/all_gather | solution.py:64
  39.6 1.4 fusion.2
  41.0 1.5 fusion.3
  42.7 0.6 broadcast_in_dim.81
  43.3 10.2 %all-to-all-start = ((s32[16,1,128]{2,1,0:T(1,128)}), s32[16,1,128]{2,1,0:T(1,128)S(1)}, u32[]{:S(2)}, u32[]{:S(2)}) async-start(s32[16,1,128]{2,1,0:T(1,128)} %broadcast_in_dim.81), calls=%async_computation | async-start | bytes 16384 | tf_op jit(solution)/shard_map/all_to_all | solution.py:23
  53.4 0.4 convolution_bitcast_fusion
  53.8 0.4 convolution_bitcast_fusion.1
  54.2 1.0 copy_bitcast_fusion
  55.2 6.7 %all-to-all-done = s32[16,1,128]{2,1,0:T(1,128)S(1)} async-done(((s32[16,1,128]{2,1,0:T(1,128)}), s32[16,1,128]{2,1,0:T(1,128)S(1)}, u32[]{:S(2)}, u32[]{:S(2)}) %all-to-all-start) | async-done | bytes 8224 | tf_op jit(solution)/shard_map/all_to_all | solution.py:23
  62.0 4.3 %all-to-all-start.4 = ((bf16[8,128,336]{1,2,0:T(8,128)(2,1)}), bf16[8,128,336]{1,2,0:T(8,128)(2,1)S(1)}, u32[]{:S(2)}, u32[]{:S(2)}) async-start(bf16[8,128,336]{1,2,0:T(8,128)(2,1)} %bitcast.24), calls=%async_computation.4 | async-start | bytes 1376256 | tf_op jit(solution)/shard_map/all_to_all | solution.py:23
  66.7 10.7 %all-to-all-done.4 = bf16[8,128,336]{1,2,0:T(8,128)(2,1)S(1)} async-done(((bf16[8,128,336]{1,2,0:T(8,128)(2,1)}), bf16[8,128,336]{1,2,0:T(8,128)(2,1)S(1)}, u32[]{:S(2)}, u32[]{:S(2)}) %all-to-all-start.4) | async-done | bytes 688160 | tf_op jit(solution)/shard_map/all_to_all | solution.py:23
  77.8 0.9 copy.68
  78.7 3.6 %all-to-all-start.5 = ((bf16[16,32,336]{2,1,0:T(8,128)(2,1)}), bf16[16,32,336]{2,1,0:T(8,128)(2,1)S(1)}, u32[]{:S(2)}, u32[]{:S(2)}) async-start(bf16[16,32,336]{2,1,0:T(8,128)(2,1)} %bitcast.25), calls=%async_computation.5 | async-start | bytes 786432 | tf_op jit(solution)/shard_map/all_to_all | solution.py:23
  82.8 8.9 %all-to-all-done.5 = bf16[16,32,336]{2,1,0:T(8,128)(2,1)S(1)} async-done(((bf16[16,32,336]{2,1,0:T(8,128)(2,1)}), bf16[16,32,336]{2,1,0:T(8,128)(2,1)S(1)}, u32[]{:S(2)}, u32[]{:S(2)}) %all-to-all-start.5) | async-done | bytes 344096 | tf_op jit(solution)/shard_map/all_to_all | solution.py:23
  91.9 0.8 copy.70
  92.8 4.8 %all-to-all-start.6 = ((bf16[16,32,336]{2,1,0:T(8,128)(2,1)}), bf16[16,32,336]{2,1,0:T(8,128)(2,1)S(1)}, u32[]{:S(2)}, u32[]{:S(2)}) async-start(bf16[16,32,336]{2,1,0:T(8,128)(2,1)} %copy.70), calls=%async_computation.6 | async-start | bytes 786432 | tf_op jit(solution)/shard_map/all_to_all | solution.py:23
  98.2 4.4 %gather_fusion = bf16[32,5376]{1,0:T(8,128)(2,1)S(1)} fusion(bf16[512,5376]{1,0:T(8,128)(2,1)} %param.6, s32[1024]{0:T(1024)S(1)} %pad_clamp_fusion), kind=kCustom, calls=%fused_computation | custom fusion | bytes 688256 | tf_op jit(solution)/shard_map/jit(_take)/gather | solution.py:71
  102.5 0.8 gather.7
  103.7 7.8 %all-to-all-done.6 = bf16[16,32,336]{2,1,0:T(8,128)(2,1)S(1)} async-done(((bf16[16,32,336]{2,1,0:T(8,128)(2,1)}), bf16[16,32,336]{2,1,0:T(8,128)(2,1)S(1)}, u32[]{:S(2)}, u32[]{:S(2)}) %all-to-all-start.6) | async-done | bytes 344096 | tf_op jit(solution)/shard_map/all_to_all | solution.py:23
  111.5 0.4 multiply_reduce_fusion
  111.8 17.0 %all_to_all.44 = bf16[16,32,336]{2,1,0:T(8,128)(2,1)S(1)} all-to-all(bf16[16,32,336]{2,1,0:T(8,128)(2,1)S(1)} %bitcast.151), channel_id=1, replica_groups=mesh['x'=4,'z_lo'=2,'core'=2,'y'=4,'z_hi'=4] {'y','z_hi'}, dimensions={0} | all-to-all | bytes 688128 | tf_op jit(solution)/shard_map/all_to_all | solution.py:23
  129.3 1.1 reshape.406
  130.4 4.6 %all-to-all-start.2 = ((bf16[16,32,336]{2,1,0:T(8,128)(2,1)}), bf16[16,32,336]{2,1,0:T(8,128)(2,1)S(1)}, u32[]{:S(2)}, u32[]{:S(2)}) async-start(bf16[16,32,336]{2,1,0:T(8,128)(2,1)} %reshape.406), calls=%async_computation.2 | async-start | bytes 786432 | tf_op jit(solution)/shard_map/all_to_all | solution.py:23
  135.0 9.4 %all-to-all-done.2 = bf16[16,32,336]{2,1,0:T(8,128)(2,1)S(1)} async-done(((bf16[16,32,336]{2,1,0:T(8,128)(2,1)}), bf16[16,32,336]{2,1,0:T(8,128)(2,1)S(1)}, u32[]{:S(2)}, u32[]{:S(2)}) %all-to-all-start.2) | async-done | bytes 344096 | tf_op jit(solution)/shard_map/all_to_all | solution.py:23
  144.4 0.3 convolution_convert_fusion.8
  144.8 27.6 %all-gather = bf16[1024,336]{0,1:T(8,128)(2,1)S(1)} all-gather(bf16[128,336]{0,1:T(8,128)(2,1)S(1)} %convolution_convert_fusion.8), channel_id=2, replica_groups=mesh['x'=4,'z_lo'=2,'core'=2,'y'=4,'z_hi'=4] {'x','z_lo'}, dimensions={0}, use_global_device_ids=true | all-gather | bytes 774144 | tf_op jit(solution)/shard_map/all_gather | solution.py:87
  172.4 1.3 reshape.408
  173.7 1.3 copy.64
  175.4 0.5 fusion.23
  176.1 0.5 convolution_add_fusion.2
  176.6 0.7 collective-permute-done
  177.5 0.5 convolution_add_fusion.1
  178.2 1.3 fusion.1
  179.5 3.7 %all-to-all-start.3 = ((bf16[4,128,512]{2,1,0:T(8,128)(2,1)}), bf16[4,128,512]{2,1,0:T(8,128)(2,1)S(1)}, u32[]{:S(2)}, u32[]{:S(2)}) async-start(bf16[4,128,512]{2,1,0:T(8,128)(2,1)} %bitcast.146), calls=%async_computation.3 | async-start | bytes 1048576 | tf_op jit(solution)/shard_map/all_to_all | solution.py:23
  183.1 1.3 fusion.4
  184.5 0.3 fusion.5
  184.8 0.3 fusion.6
  185.9 1.2 pad_maximum_fusion
  187.2 11.5 %all-to-all-done.3 = bf16[4,128,512]{2,1,0:T(8,128)(2,1)S(1)} async-done(((bf16[4,128,512]{2,1,0:T(8,128)(2,1)}), bf16[4,128,512]{2,1,0:T(8,128)(2,1)S(1)}, u32[]{:S(2)}, u32[]{:S(2)}) %all-to-all-start.3) | async-done | bytes 524320 | tf_op jit(solution)/shard_map/all_to_all | solution.py:23
  198.7 6.0 %all-to-all-start.7 = ((bf16[4,336,512]{2,1,0:T(8,128)(2,1)}), bf16[4,336,512]{2,1,0:T(8,128)(2,1)S(1)}, u32[]{:S(2)}, u32[]{:S(2)}) async-start(bf16[4,336,512]{2,1,0:T(8,128)(2,1)} %bitcast.35), calls=%async_computation.7 | async-start | bytes 2752512 | tf_op jit(solution)/shard_map/all_to_all | solution.py:23
  204.9 0.5 copy.71
  205.4 1.5 reshape.417
  206.8 5.2 %convolution_convert_fusion = bf16[512,5376]{1,0:T(8,128)(2,1)} fusion(f32[32,5376]{1,0:T(8,128)} %reshape.417, f32[32]{0:T(128)S(1)} %div.42, f32[5376]{0:T(1024)S(1)} %convert_element_type.79, f32[32]{0:T(128)S(1)} %add_rsqrt_fusion, s32[32]{0:T(128)S(1)} %reshape.403, bf16[32,5376]{1,0:T(8,128)(2,1)S(1)} %gather_fusion, ...), kind=kOutput, calls=%fused_computation.1 | convolution fusion | flops 180477952 | bytes 6559168 | tf_op jit(solution)/shard_map/dot_general | solution.py:15
  212.0 0.7 reduce_sum.85
  212.8 8.5 %all-to-all-done.7 = bf16[4,336,512]{2,1,0:T(8,128)(2,1)S(1)} async-done(((bf16[4,336,512]{2,1,0:T(8,128)(2,1)}), bf16[4,336,512]{2,1,0:T(8,128)(2,1)S(1)}, u32[]{:S(2)}, u32[]{:S(2)}) %all-to-all-start.7) | async-done | bytes 1376288 | tf_op jit(solution)/shard_map/all_to_all | solution.py:23
  221.3 1.0 reduce_sum.88
  (57 shorter events, 5.1 us)
Async XLA Ops:
  7.2 32.4 %all-gather.4.cloned.1.call-start = ((), (), s32[]{:S(2)}) async-start(), calls=%async_computation.8 | async-start | bytes 1720320 | tf_op jit(solution)/shard_map/all_gather | solution.py:64
  41.0 1.7 copy-start.5
  41.0 1.7 copy-start.6
  41.0 12.5 %copy-start = (bf16[1344,512]{1,0:T(8,128)(2,1)S(1)}, bf16[1344,512]{1,0:T(8,128)(2,1)}, u32[]{:S(2)}) copy-start(bf16[1344,512]{1,0:T(8,128)(2,1)} %all-gather.4.cloned.1.call-done) | copy-start | bytes 4128772
  42.5 11.7 %collective-permute-start.1 = (bf16[2,512,336]{1,2,0:T(8,128)(2,1)S(1)}, bf16[2,512,336]{1,2,0:T(8,128)(2,1)S(1)}, u32[]{:S(2)}, u32[]{:S(2)}) collective-permute-start(bf16[2,512,336]{1,2,0:T(8,128)(2,1)S(1)} %pad_maximum_fusion.1), channel_id=1, source_target_pairs={{0,16},{16,0},{1,17},{17,1},{2,18},{18,2},{3,19},{19,3},{4,20},{20... | collective-permute-start | bytes 2064392 | tf_op jit(solution)/shard_map/ppermute | solution.py:19
  43.3 18.7 %all-to-all-start = ((s32[16,1,128]{2,1,0:T(1,128)}), s32[16,1,128]{2,1,0:T(1,128)S(1)}, u32[]{:S(2)}, u32[]{:S(2)}) async-start(s32[16,1,128]{2,1,0:T(1,128)} %broadcast_in_dim.81), calls=%async_computation | async-start | bytes 16384 | tf_op jit(solution)/shard_map/all_to_all | solution.py:23
  55.2 11.1 %copy-start.4 = (bf16[5376]{0:T(1024)(128)(2,1)S(1)}, bf16[5376]{0:T(1024)(128)(2,1)}, u32[]{:S(2)}) copy-start(bf16[5376]{0:T(1024)(128)(2,1)} %param.9) | copy-start | bytes 32260
  62.0 15.4 %all-to-all-start.4 = ((bf16[8,128,336]{1,2,0:T(8,128)(2,1)}), bf16[8,128,336]{1,2,0:T(8,128)(2,1)S(1)}, u32[]{:S(2)}, u32[]{:S(2)}) async-start(bf16[8,128,336]{1,2,0:T(8,128)(2,1)} %bitcast.24), calls=%async_computation.4 | async-start | bytes 1376256 | tf_op jit(solution)/shard_map/all_to_all | solution.py:23
  78.7 13.0 %all-to-all-start.5 = ((bf16[16,32,336]{2,1,0:T(8,128)(2,1)}), bf16[16,32,336]{2,1,0:T(8,128)(2,1)S(1)}, u32[]{:S(2)}, u32[]{:S(2)}) async-start(bf16[16,32,336]{2,1,0:T(8,128)(2,1)} %bitcast.25), calls=%async_computation.5 | async-start | bytes 786432 | tf_op jit(solution)/shard_map/all_to_all | solution.py:23
  92.8 18.7 %all-to-all-start.6 = ((bf16[16,32,336]{2,1,0:T(8,128)(2,1)}), bf16[16,32,336]{2,1,0:T(8,128)(2,1)S(1)}, u32[]{:S(2)}, u32[]{:S(2)}) async-start(bf16[16,32,336]{2,1,0:T(8,128)(2,1)} %copy.70), calls=%async_computation.6 | async-start | bytes 786432 | tf_op jit(solution)/shard_map/all_to_all | solution.py:23
  130.4 14.0 %all-to-all-start.2 = ((bf16[16,32,336]{2,1,0:T(8,128)(2,1)}), bf16[16,32,336]{2,1,0:T(8,128)(2,1)S(1)}, u32[]{:S(2)}, u32[]{:S(2)}) async-start(bf16[16,32,336]{2,1,0:T(8,128)(2,1)} %reshape.406), calls=%async_computation.2 | async-start | bytes 786432 | tf_op jit(solution)/shard_map/all_to_all | solution.py:23
  175.0 2.2 collective-permute-start
  175.4 0.7 copy-start.1
  177.5 0.7 copy-start.2
  179.5 19.2 %all-to-all-start.3 = ((bf16[4,128,512]{2,1,0:T(8,128)(2,1)}), bf16[4,128,512]{2,1,0:T(8,128)(2,1)S(1)}, u32[]{:S(2)}, u32[]{:S(2)}) async-start(bf16[4,128,512]{2,1,0:T(8,128)(2,1)} %bitcast.146), calls=%async_computation.3 | async-start | bytes 1048576 | tf_op jit(solution)/shard_map/all_to_all | solution.py:23
  184.5 1.0 copy-start.3
  198.7 22.6 %all-to-all-start.7 = ((bf16[4,336,512]{2,1,0:T(8,128)(2,1)}), bf16[4,336,512]{2,1,0:T(8,128)(2,1)S(1)}, u32[]{:S(2)}, u32[]{:S(2)}) async-start(bf16[4,336,512]{2,1,0:T(8,128)(2,1)} %bitcast.35), calls=%async_computation.7 | async-start | bytes 2752512 | tf_op jit(solution)/shard_map/all_to_all | solution.py:23
Sparse Core Ops, SparseCore 0:
  9.8 29.7 all-gather.3

commit v2 on v1

v2 whole, which is shorter than its diff:
```python
import jax
import jax.numpy as jnp
from jax import lax
from jax.sharding import Mesh, PartitionSpec as P

EPS = 1e-06
SECTION = ("x", "z_lo", "core")
SEQ = ("y", "z_hi")
CAP = 2
BF16 = jnp.bfloat16
F32 = jnp.float32


def dot(a, b, contract):
    return lax.dot_general(a, b, (contract, ((), ())), preferred_element_type=F32)


def shift(x, axis, by):
    size = lax.axis_size(axis)
    return lax.ppermute(x, axis, [(i, (i + by) % size) for i in range(size)])


def exchange(x, axes):
    return lax.all_to_all(x, axes, split_axis=0, concat_axis=0, tiled=True)


def pick(x, index):
    return lax.dynamic_index_in_dim(x, index, 0, keepdims=False)


def sum_f32(parts):
    total = parts[0].astype(F32)
    for part in parts[1:]:
        total = total + part.astype(F32)
    return total


def owner_rows(token_ids, shard, vocab_rows):
    tokens = token_ids.shape[1]
    mine = token_ids // vocab_rows == shard
    place = jnp.arange(tokens, dtype=jnp.int32)[None, :]
    first = jnp.min(jnp.where(mine, place, tokens), axis=1, keepdims=True)
    last = jnp.max(jnp.where(mine, place, -1), axis=1, keepdims=True)
    row = token_ids % vocab_rows
    row_first = jnp.sum(jnp.where(place == first, row, 0), axis=1)
    row_last = jnp.sum(jnp.where(place == last, row, 0), axis=1)
    some = last[:, 0] >= 0
    two = jnp.logical_and(some, last[:, 0] != first[:, 0])
    return jnp.stack([jnp.where(some, row_first, -1), jnp.where(two, row_last, -1)], axis=1)


def token_slots(block_ids, vocab_rows):
    shard = block_ids // vocab_rows
    place = jnp.arange(shard.shape[0], dtype=jnp.int32)
    earlier = jnp.logical_and(shard[:, None] == shard[None, :], place[None, :] < place[:, None])
    return shard * CAP + jnp.sum(earlier.astype(jnp.int32), axis=1)


def per_device(embed_table, vocab_shard, shard_row, norm_gain, weight, cotangent):
    nx, nzl, nc = (lax.axis_size(a) for a in SECTION)
    ny, nzh = (lax.axis_size(a) for a in SEQ)
    n_section, n_seq = nx * nzl * nc, ny * nzh
    vocab_rows, model_width = embed_table.shape
    tok = shard_row.shape[0]
    feat, cols = weight.shape
    section, seq = lax.axis_index(SECTION), lax.axis_index(SEQ)
    ix, iz, ic, iy, ih = (lax.axis_index(a) for a in SECTION + SEQ)
    nb, nf = nx, nzl * nc
    block_slots = n_seq * CAP
    slots = n_section * block_slots

    ids = vocab_shard[:, 0] * vocab_rows + shard_row
    all_ids = exchange(jnp.broadcast_to(ids[None], (n_seq, tok)), SEQ)

    cot = [shift(cotangent, "z_hi", d) for d in range(nzh - 1, 0, -1)] + [cotangent]
    cot, all_ids = lax.optimization_barrier((jnp.stack(cot + cot), all_ids))
    cot = lax.dynamic_slice_in_dim(cot, (ix - ih) % nx, nx, 0)[::-1]
    cot = cot.reshape(nx * tok, cols)

    w = jnp.stack([weight] + [shift(weight, "y", d) for d in range(1, ny)])
    w = [
        jnp.concatenate([pick(w, (iy - (iz ^ z) * nc - (ic ^ c)) % ny) for z in range(nzl)], axis=0)
        for c in range(nc)
    ]

    wanted = owner_rows(all_ids, section * n_seq + seq, vocab_rows).reshape(-1)
    pick_matrix = (jnp.arange(vocab_rows, dtype=jnp.int32)[:, None] == wanted[None, :]).astype(BF16)
    embedded = dot(pick_matrix, embed_table, ((0,), (0,)))
    inv_rms = lax.rsqrt(jnp.mean(embedded * embedded, axis=-1, keepdims=True) + EPS)
    unit_rows = embedded * inv_rms
    gain_full = norm_gain.astype(F32)
    normed_rows = (unit_rows * gain_full).astype(BF16)

    out_rows = normed_rows.reshape(ny, nb * CAP, nf, nzh, feat).transpose(0, 3, 2, 1, 4)
    got = exchange(out_rows.reshape(n_seq, nf * nb * CAP, feat), SEQ)
    got = got.reshape(n_seq, nf, nb, CAP, feat).transpose(2, 1, 0, 3, 4)
    got = exchange(got.reshape(n_section, block_slots, feat), SECTION)
    block_ids = pick(all_ids, iy * nzh + ix)
    slot = token_slots(block_ids, vocab_rows)
    place = (jnp.arange(slots, dtype=jnp.int32)[:, None] == slot[None, :]).astype(BF16)
    normed = dot(got.reshape(slots, feat), place, ((0,), (0,))).astype(BF16)

    normed = jnp.concatenate([normed, shift(normed, "z_lo", 1)], axis=0)
    normed = jnp.concatenate([normed] + [shift(normed, "x", e) for e in range(1, nx)], axis=1)
    n_half = [normed, shift(normed, "core", 1)]

    up_keep = dot(w[0], cot, ((1,), (1,)))
    up_send = dot(w[1], cot, ((1,), (1,))).astype(BF16)
    up = (up_keep + shift(up_send, "core", 1).astype(F32)).astype(BF16)
    up = up.reshape(nzl * feat, nx, tok)
    up = sum_f32([up[:, 0]] + [shift(up[:, e], "x", -e) for e in range(1, nx)])
    up = (up[:feat] + shift(up[feat:].astype(BF16), "z_lo", 1).astype(F32)).astype(BF16)
    after = slot + (got[0, 0, 0].astype(F32) * 0.0).astype(jnp.int32)
    place_back = (jnp.arange(slots, dtype=jnp.int32)[:, None] == after[None, :]).astype(BF16)
    back = dot(place_back, up, ((1,), (1,))).astype(BF16).reshape(n_section, block_slots, feat)
    back = exchange(back, SECTION).reshape(nb, nf, n_seq, CAP, feat).transpose(2, 1, 0, 3, 4)
    back = exchange(back.reshape(n_seq, nf * nb * CAP, feat), SEQ)
    back = back.reshape(ny, nzh, nf, nb * CAP, feat).transpose(0, 3, 2, 1, 4)
    upstream = back.reshape(n_seq * CAP, model_width).astype(F32)
    scaled = upstream * gain_full
    row_grads = (
        inv_rms * (scaled - unit_rows * jnp.mean(scaled * unit_rows, axis=-1, keepdims=True))
    ).astype(BF16)
    table_grad = dot(pick_matrix, row_grads, ((1,), (0,))).astype(BF16)

    proj = sum(dot(n, w[c], ((0,), (0,))) for c, n in enumerate(n_half))
    proj = proj.astype(BF16).reshape(nx, tok, cols)
    proj = [pick(proj, (ix - ih - d) % nx) for d in range(nzh)]
    projected = sum_f32([proj[0]] + [shift(proj[d], "z_hi", d) for d in range(1, nzh)]).astype(BF16)

    grad = jnp.concatenate([dot(n, cot, ((1,), (0,))).astype(BF16) for n in n_half], axis=0)
    grad = grad.reshape(nf, feat, cols)

    def slice_for(d):
        f = (iy + d) % ny
        return pick(grad, (ic ^ (f % nc)) * nzl + (iz ^ (f // nc)))
    weight_grad = sum_f32(
        [slice_for(0)] + [shift(slice_for(d), "y", d) for d in range(1, ny)]
    ).astype(BF16)
    return projected, table_grad, weight_grad


def solution(mesh):
    devices = mesh.devices.reshape(4, 2, 2, 4, 4)
    fine = Mesh(devices, SECTION + SEQ)
    in_specs = (
        P(SECTION + SEQ, None),
        P(SEQ, None),
        P(SEQ),
        P(),
        P(SEQ, SECTION),
        P(SEQ, SECTION),
    )
    out_specs = (P(SEQ, SECTION), P(SECTION + SEQ, None), P(SEQ, SECTION))
    return jax.shard_map(
        per_device, mesh=fine, in_specs=in_specs, out_specs=out_specs, check_vma=False
    )
```

time: 231 us -> 151 us (0.65)
  blocking collectives: 64.9 us -> 0 us
  waiting for transfers between devices: 76.3 us -> 47.9 us
  starting transfers between devices: 37.3 us -> 62.7 us
  between operations: 14.4 us -> 2.15 us
  local copies, waits for them, and re-layouts: 16.1 us -> 11.8 us
  matrix products: 14.4 us -> 17.3 us
    all_gather x2 -> x0, blocking collectives: 47.9 us -> none  [the longest x1 27.6 us: per_device(): lax.all_gather(normed_block, ('x', 'z_lo'), axis=0)]
    all_to_all x7 -> x5, waiting for transfers between devices: 63.5 us -> 27.2 us  [exchange(): return lax.all_to_all(x, axes, split_axis=0, concat_axis=0, tiled=True)]
    ppermute x2 -> x22, starting transfers between devices: 0.19 us -> 36.4 us  [shift(): return lax.ppermute(x, axis, [(i, (i + by) % size) for i in range(size)])]
    ppermute x2 -> x22, waiting for transfers between devices: 0.68 us -> 20.7 us  [shift(): return lax.ppermute(x, axis, [(i, (i + by) % size) for i in range(size)])]
    all_to_all x1 -> x0, blocking collectives: 17 us -> none  [exchange(): return lax.all_to_all(x, axes, split_axis=0, concat_axis=0, tiled=True)]
    all_gather x1 -> x0, waiting for transfers between devices: 11.4 us -> none  [per_device(): w_y = lax.all_gather(weight, 'y', axis=0)]
    all_to_all x7 -> x5, starting transfers between devices: 37.1 us -> 26.4 us  [exchange(): return lax.all_to_all(x, axes, split_axis=0, concat_axis=0, tiled=True)]
    gather x2 -> x0, local copies, waits for them, and re-layouts: 5.12 us -> none  [per_device(): found = jnp.take(embed_table, jnp.maximum(wanted, 0), axis=0)]
  transfers between devices with their start and end apart: 10 -> 27, of which waited for: 9 -> 10; matrix products, arithmetic and copies ran while one was open for 10% -> 22% of each run, Pallas kernels for 0% -> 0%
where the time goes in v2:
time: 151 us; the launch traced here: 149 us
  starting transfers between devices  62.7 us (42%)
  waiting for transfers between devices  47.9 us (32%)
  matrix products  17.3 us (11%)
  local copies, waits for them, and re-layouts  11.8 us (8%)
  other arithmetic  7.45 us (5%)
  between operations  2.15 us (1%)
    ppermute x22, starting transfers between devices, shift(): return lax.ppermute(x, axis, [(i, (i + by) % size) for i in range(size)])  36.4 us
    all_to_all x5, waiting for transfers between devices, exchange(): return lax.all_to_all(x, axes, split_axis=0, concat_axis=0, tiled=True)  27.2 us
    all_to_all x5, starting transfers between devices, exchange(): return lax.all_to_all(x, axes, split_axis=0, concat_axis=0, tiled=True)  26.4 us
    ppermute x22, waiting for transfers between devices, shift(): return lax.ppermute(x, axis, [(i, (i + by) % size) for i in range(size)])  20.7 us
    dot_general x10, matrix products, dot(): lax.dot_general(a, b, (contract, ((), ())), preferred_element_type=F32)  17.3 us
  transfers between devices with their start and end apart: 27, of which 10 were waited for; matrix products, arithmetic and copies ran while one was open for 22% of the time, Pallas kernels for 0%

profile of v2, /device:TPU:8, one launch (start us, length us, event | category | flops | bytes accessed | tf_op | source)
XLA Modules:
  0.0 149.3 jit_solution(17864129378095539530)
XLA Ops:
  0.6 7.3 %collective-permute-start.1 = (bf16[128,512]{1,0:T(8,128)(2,1)}, bf16[128,512]{1,0:T(8,128)(2,1)S(1)}, u32[]{:S(2)}, u32[]{:S(2)}) collective-permute-start(bf16[128,512]{1,0:T(8,128)(2,1)} %param.11), channel_id=1, source_target_pairs={{0,2},{1,3},{2,0},{3,1},{4,6},{5,7},{6,4},{7,5},{8,10},{9,11},{10,... | collective-permute-start | bytes 393224 | tf_op jit(solution)/shard_map/ppermute | solution.py:20
  7.9 2.9 %collective-permute-start.2 = (bf16[128,512]{1,0:T(8,128)(2,1)}, bf16[128,512]{1,0:T(8,128)(2,1)S(1)}, u32[]{:S(2)}, u32[]{:S(2)}) collective-permute-start(bf16[128,512]{1,0:T(8,128)(2,1)} %param.11), channel_id=1, source_target_pairs={{0,1},{1,2},{2,3},{3,0},{4,5},{5,6},{6,7},{7,4},{8,9},{9,10},{10,1... | collective-permute-start | bytes 393224 | tf_op jit(solution)/shard_map/ppermute | solution.py:20
  10.8 1.6 %collective-permute-start.7 = (bf16[336,512]{1,0:T(8,128)(2,1)}, bf16[336,512]{1,0:T(8,128)(2,1)S(1)}, u32[]{:S(2)}, u32[]{:S(2)}) collective-permute-start(bf16[336,512]{1,0:T(8,128)(2,1)} %param.10), channel_id=1, source_target_pairs={{0,4},{4,8},{8,12},{12,0},{1,5},{5,9},{9,13},{13,1},{2,6},{6,10},{... | collective-permute-start | bytes 1032200 | tf_op jit(solution)/shard_map/ppermute | solution.py:20
  14.2 7.1 %all-to-all-start = ((s32[16,1,128]{2,1,0:T(1,128)}), s32[16,1,128]{2,1,0:T(1,128)S(1)}, u32[]{:S(2)}, u32[]{:S(2)}) async-start(s32[16,1,128]{2,1,0:T(1,128)} %broadcast_in_dim.52), calls=%async_computation | async-start | bytes 16384 | tf_op jit(solution)/shard_map/all_to_all | solution.py:24
  21.2 0.7 convert_element_type.122
  21.9 2.2 %collective-permute-start.8 = (bf16[336,512]{1,0:T(8,128)(2,1)}, bf16[336,512]{1,0:T(8,128)(2,1)}, u32[]{:S(2)}, u32[]{:S(2)}) collective-permute-start(bf16[336,512]{1,0:T(8,128)(2,1)} %param.10), channel_id=1, source_target_pairs={{0,8},{4,12},{8,0},{12,4},{1,9},{5,13},{9,1},{13,5},{2,10},{6,14},... | collective-permute-start | bytes 1032200 | tf_op jit(solution)/shard_map/ppermute | solution.py:20
  24.1 0.9 bitcast_dynamic-update-slice_fusion
  25.2 4.6 %all-to-all-done = s32[16,1,128]{2,1,0:T(1,128)S(1)} async-done(((s32[16,1,128]{2,1,0:T(1,128)}), s32[16,1,128]{2,1,0:T(1,128)S(1)}, u32[]{:S(2)}, u32[]{:S(2)}) %all-to-all-start) | async-done | bytes 8224 | tf_op jit(solution)/shard_map/all_to_all | solution.py:24
  30.2 3.7 %multiply_reduce_fusion.1 = (f32[32]{0:T(128)S(1)}, f32[32,5376]{1,0:T(8,128)S(1)}) fusion(bf16[512,5376]{1,0:T(8,128)(2,1)} %param.6, s32[32]{0:T(128)S(1)} %eq.115), kind=kOutput, calls=%fused_computation.22 | convolution fusion | flops 176521184 | bytes 6193408 | tf_op jit(solution)/shard_map/dot_general | solution.py:15
  34.3 0.8 reshape.155
  35.0 0.8 copy.36
  35.9 4.8 %all-to-all-start.1 = ((bf16[16,32,336]{2,1,0:T(8,128)(2,1)}), bf16[16,32,336]{2,1,0:T(8,128)(2,1)S(1)}, u32[]{:S(2)}, u32[]{:S(2)}) async-start(bf16[16,32,336]{2,1,0:T(8,128)(2,1)} %bitcast.9), calls=%async_computation.1 | async-start | bytes 786432 | tf_op jit(solution)/shard_map/all_to_all | solution.py:24
  40.7 1.2 pad_maximum_fusion
  41.9 0.8 dynamic-slice_bitcast_fusion.6
  42.7 1.4 convolution_convert_fusion.3
  44.1 7.7 %all-to-all-done.1 = bf16[16,32,336]{2,1,0:T(8,128)(2,1)S(1)} async-done(((bf16[16,32,336]{2,1,0:T(8,128)(2,1)}), bf16[16,32,336]{2,1,0:T(8,128)(2,1)S(1)}, u32[]{:S(2)}, u32[]{:S(2)}) %all-to-all-start.1) | async-done | bytes 344096 | tf_op jit(solution)/shard_map/all_to_all | solution.py:24
  52.3 1.1 reshape.158
  53.4 5.1 %all-to-all-start.2 = ((bf16[16,32,336]{2,1,0:T(8,128)(2,1)}), bf16[16,32,336]{2,1,0:T(8,128)(2,1)S(1)}, u32[]{:S(2)}, u32[]{:S(2)}) async-start(bf16[16,32,336]{2,1,0:T(8,128)(2,1)} %reshape.158), calls=%async_computation.2 | async-start | bytes 786432 | tf_op jit(solution)/shard_map/all_to_all | solution.py:24
  58.8 1.8 %add_convert_fusion = bf16[672,512]{1,0:T(8,128)(2,1)S(1)} fusion(bf16[672,512]{1,0:T(8,128)(2,1)} %collective-permute-done.14, bf16[512,512]{1,0:T(8,128)(2,1)S(1)} %bitcast.116, bf16[336,512]{1,0:T(8,128)(2,1)} %get-tuple-element.17, bf16[336,512]{1,0:T(8,128)(2,1)S(1)} %get-tuple-element.14), kind=kOutput, calls=%fused_computation.3 | convolution fusion | flops 354729984 | bytes 2588672 | tf_op jit(solution)/shard_map/dot_general | solution.py:15
  60.7 7.3 %all-to-all-done.2 = bf16[16,32,336]{2,1,0:T(8,128)(2,1)S(1)} async-done(((bf16[16,32,336]{2,1,0:T(8,128)(2,1)}), bf16[16,32,336]{2,1,0:T(8,128)(2,1)S(1)}, u32[]{:S(2)}, u32[]{:S(2)}) %all-to-all-start.2) | async-done | bytes 344096 | tf_op jit(solution)/shard_map/all_to_all | solution.py:24
  69.5 0.9 collective-permute-start.3
  70.4 1.0 fusion.32
  71.7 3.2 %collective-permute-start.15 = (bf16[672,128]{1,0:T(8,128)(2,1)S(1)}, bf16[672,128]{1,0:T(8,128)(2,1)S(1)}, u32[]{:S(2)}, u32[]{:S(2)}) collective-permute-start(bf16[672,128]{1,0:T(8,128)(2,1)S(1)} %bitcast.126), channel_id=1, source_target_pairs={{0,192},{64,0},{128,64},{192,128},{1,193},{65,1},{129,65},{193,129... | collective-permute-start | bytes 516104 | tf_op jit(solution)/shard_map/ppermute | solution.py:20
  75.0 1.6 %collective-permute-start.6 = (bf16[672,128]{1,0:T(8,128)(2,1)S(1)}, bf16[672,128]{1,0:T(8,128)(2,1)S(1)}, u32[]{:S(2)}, u32[]{:S(2)}) collective-permute-start(bf16[672,128]{1,0:T(8,128)(2,1)S(1)} %pad_maximum_fusion.11), channel_id=1, source_target_pairs={{0,192},{64,0},{128,64},{192,128},{1,193},{65,1},{129,65},{193,129... | collective-permute-start | bytes 516104 | tf_op jit(solution)/shard_map/ppermute | solution.py:20
  76.6 2.1 %collective-permute-start.5 = (bf16[672,128]{1,0:T(8,128)(2,1)S(1)}, bf16[672,128]{1,0:T(8,128)(2,1)S(1)}, u32[]{:S(2)}, u32[]{:S(2)}) collective-permute-start(bf16[672,128]{1,0:T(8,128)(2,1)S(1)} %pad_maximum_fusion.11), channel_id=1, source_target_pairs={{0,128},{64,192},{128,0},{192,64},{1,129},{65,193},{129,1},{193,65... | collective-permute-start | bytes 516104 | tf_op jit(solution)/shard_map/ppermute | solution.py:20
  78.7 7.8 %collective-permute-done.17 = bf16[672,128]{1,0:T(8,128)(2,1)S(1)} collective-permute-done((bf16[672,128]{1,0:T(8,128)(2,1)S(1)}, bf16[672,128]{1,0:T(8,128)(2,1)S(1)}, u32[]{:S(2)}, u32[]{:S(2)}) %collective-permute-start.17) | collective-permute-done | bytes 172064 | tf_op jit(solution)/shard_map/ppermute | solution.py:20
  86.7 2.7 %collective-permute-done.6 = bf16[672,128]{1,0:T(8,128)(2,1)S(1)} collective-permute-done((bf16[672,128]{1,0:T(8,128)(2,1)S(1)}, bf16[672,128]{1,0:T(8,128)(2,1)S(1)}, u32[]{:S(2)}, u32[]{:S(2)}) %collective-permute-start.6) | collective-permute-done | bytes 172064 | tf_op jit(solution)/shard_map/ppermute | solution.py:20
  89.4 3.7 %collective-permute-done.4 = bf16[672,128]{1,0:T(8,128)(2,1)S(1)} collective-permute-done((bf16[672,128]{1,0:T(8,128)(2,1)S(1)}, bf16[672,128]{1,0:T(8,128)(2,1)S(1)}, u32[]{:S(2)}, u32[]{:S(2)}) %collective-permute-start.4) | collective-permute-done | bytes 172064 | tf_op jit(solution)/shard_map/ppermute | solution.py:20
  93.6 0.9 copy.42
  94.5 3.6 %all-to-all-start.3 = ((bf16[16,32,336]{2,1,0:T(8,128)(2,1)}), bf16[16,32,336]{2,1,0:T(8,128)(2,1)S(1)}, u32[]{:S(2)}, u32[]{:S(2)}) async-start(bf16[16,32,336]{2,1,0:T(8,128)(2,1)} %bitcast.36), calls=%async_computation.3 | async-start | bytes 786432 | tf_op jit(solution)/shard_map/all_to_all | solution.py:24
  98.3 1.5 %convolution_convert_fusion.2 = bf16[672,512]{1,0:T(8,128)(2,1)S(1)} fusion(bf16[512,512]{1,0:T(8,128)(2,1)S(1)} %bitcast.117, bf16[672,128]{1,0:T(8,128)(2,1)S(1)} %collective-permute-done.6, bf16[672,128]{1,0:T(8,128)(2,1)} %copy-done.13, bf16[672,128]{1,0:T(8,128)(2,1)} %copy-done.15, bf16[336,128]{1,0:T(8,128)(2,1)S(1)} %collective-permute-done.3, ...), kind=kOutput, calls=%fused_computation.6 | convolution fusion | flops 356106240 | bytes 1900544 | tf_op jit(solution)/shard_map/dot_general | solution.py:15
  99.8 7.6 %all-to-all-done.3 = bf16[16,32,336]{2,1,0:T(8,128)(2,1)S(1)} async-done(((bf16[16,32,336]{2,1,0:T(8,128)(2,1)}), bf16[16,32,336]{2,1,0:T(8,128)(2,1)S(1)}, u32[]{:S(2)}, u32[]{:S(2)}) %all-to-all-start.3) | async-done | bytes 344096 | tf_op jit(solution)/shard_map/all_to_all | solution.py:24
  107.7 0.8 copy.44
  108.5 5.8 %all-to-all-start.4 = ((bf16[16,32,336]{2,1,0:T(8,128)(2,1)}), bf16[16,32,336]{2,1,0:T(8,128)(2,1)S(1)}, u32[]{:S(2)}, u32[]{:S(2)}) async-start(bf16[16,32,336]{2,1,0:T(8,128)(2,1)} %copy.44), calls=%async_computation.4 | async-start | bytes 786432 | tf_op jit(solution)/shard_map/all_to_all | solution.py:24
  114.4 2.0 %fusion.4 = f32[512,512]{1,0:T(8,128)S(1)} fusion(bf16[672,512]{1,0:T(8,128)(2,1)} %collective-permute-done.10, bf16[336,512]{1,0:T(8,128)(2,1)} %copy-done.6, bf16[336,512]{1,0:T(8,128)(2,1)} %copy-done.7), kind=kOutput, calls=%fused_computation.23 | convolution fusion | flops 353697792 | bytes 2424832 | tf_op jit(solution)/shard_map/dot_general | solution.py:15
  117.1 2.4 %collective-permute-start.11 = (bf16[128,512]{1,0:T(8,128)(2,1)S(1)}, bf16[128,512]{1,0:T(8,128)(2,1)S(1)}, u32[]{:S(2)}, u32[]{:S(2)}) collective-permute-start(bf16[128,512]{1,0:T(8,128)(2,1)S(1)} %get-tuple-element.22), channel_id=1, source_target_pairs={{0,1},{1,2},{2,3},{3,0},{4,5},{5,6},{6,7},{7,4},{8,9},{9,10},{10,1... | collective-permute-start | bytes 393224 | tf_op jit(solution)/shard_map/ppermute | solution.py:20
  119.6 1.8 %collective-permute-start.13 = (bf16[128,512]{1,0:T(8,128)(2,1)S(1)}, bf16[128,512]{1,0:T(8,128)(2,1)S(1)}, u32[]{:S(2)}, u32[]{:S(2)}) collective-permute-start(bf16[128,512]{1,0:T(8,128)(2,1)S(1)} %get-tuple-element.23), channel_id=1, source_target_pairs={{0,3},{1,0},{2,1},{3,2},{4,7},{5,4},{6,5},{7,6},{8,11},{9,8},{10,9... | collective-permute-start | bytes 393224 | tf_op jit(solution)/shard_map/ppermute | solution.py:20
  121.4 5.4 %collective-permute-start.12 = (bf16[128,512]{1,0:T(8,128)(2,1)S(1)}, bf16[128,512]{1,0:T(8,128)(2,1)S(1)}, u32[]{:S(2)}, u32[]{:S(2)}) collective-permute-start(bf16[128,512]{1,0:T(8,128)(2,1)S(1)} %get-tuple-element.24), channel_id=1, source_target_pairs={{0,2},{1,3},{2,0},{3,1},{4,6},{5,7},{6,4},{7,5},{8,10},{9,11},{10,... | collective-permute-start | bytes 393224 | tf_op jit(solution)/shard_map/ppermute | solution.py:20
  126.7 1.6 %convolution_convert_fusion.1 = bf16[672,512]{1,0:T(8,128)(2,1)S(1)} fusion(bf16[672,512]{1,0:T(8,128)(2,1)} %collective-permute-done.10, bf16[512,512]{1,0:T(8,128)(2,1)S(1)} %bitcast.118), kind=kOutput, calls=%fused_computation.5 | convolution fusion | flops 352665600 | bytes 1900544 | tf_op jit(solution)/shard_map/dot_general | solution.py:15
  128.5 1.0 dynamic-slice_bitcast_fusion.2
  129.5 1.5 collective-permute-start.19
  131.5 2.1 %collective-permute-start.20 = (bf16[336,512]{1,0:T(8,128)(2,1)}, bf16[336,512]{1,0:T(8,128)(2,1)}, u32[]{:S(2)}, u32[]{:S(2)}) collective-permute-start(bf16[336,512]{1,0:T(8,128)(2,1)} %get-tuple-element.13), channel_id=1, source_target_pairs={{0,8},{4,12},{8,0},{12,4},{1,9},{5,13},{9,1},{13,5},{2,10},{6,14},... | collective-permute-start | bytes 1032200 | tf_op jit(solution)/shard_map/ppermute | solution.py:20
  133.6 3.1 %collective-permute-done.13 = bf16[128,512]{1,0:T(8,128)(2,1)S(1)} collective-permute-done((bf16[128,512]{1,0:T(8,128)(2,1)S(1)}, bf16[128,512]{1,0:T(8,128)(2,1)S(1)}, u32[]{:S(2)}, u32[]{:S(2)}) %collective-permute-start.13) | collective-permute-done | bytes 131104 | tf_op jit(solution)/shard_map/ppermute | solution.py:20
  136.7 2.8 %collective-permute-done.12 = bf16[128,512]{1,0:T(8,128)(2,1)S(1)} collective-permute-done((bf16[128,512]{1,0:T(8,128)(2,1)S(1)}, bf16[128,512]{1,0:T(8,128)(2,1)S(1)}, u32[]{:S(2)}, u32[]{:S(2)}) %collective-permute-start.12) | collective-permute-done | bytes 131104 | tf_op jit(solution)/shard_map/ppermute | solution.py:20
  139.5 0.7 fusion.13
  141.5 1.0 multiply_reduce_fusion
  142.5 4.1 %convolution_convert_fusion = bf16[512,5376]{1,0:T(8,128)(2,1)} fusion(f32[32,5376]{1,0:T(8,128)S(1)} %reshape.169, f32[32,5376]{1,0:T(8,128)S(1)} %get-tuple-element.30, f32[32]{0:T(128)S(1)} %broadcast_multiply_fusion, f32[5376]{0:T(1024)S(1)} %copy-done.2, f32[32]{0:T(128)S(1)} %add_rsqrt_fusion, s32[32]{0:T(128)S(1)} %eq.115), kind=kOutput, calls=%fused_computation | convolution fusion | flops 179961856 | bytes 6903168 | tf_op jit(solution)/shard_map/dot_general | solution.py:15
  147.2 2.1 %fusion.3 = bf16[336,512]{1,0:T(8,128)(2,1)} fusion(bf16[336,512]{1,0:T(8,128)(2,1)} %collective-permute-done.21, bf16[336,512]{1,0:T(8,128)(2,1)} %collective-permute-done.20, bf16[336,512]{1,0:T(8,128)(2,1)} %collective-permute-done.19, bf16[4,336,512]{2,1,0:T(8,128)(2,1)S(1)} %bitcast.110, s32[]{:T(128)S(6)} %select_n.226), kind=kLoop, calls=%fused_computation.18 | loop fusion | flops 1376256 | bytes 1720324 | tf_op jit(solution)/shard_map/convert_element_type | solution.py:139
  (106 shorter events, 8.5 us)
Async XLA Ops:
  0.6 24.5 %copy-start = (bf16[128,512]{1,0:T(8,128)(2,1)S(1)}, bf16[128,512]{1,0:T(8,128)(2,1)}, u32[]{:S(2)}) copy-start(bf16[128,512]{1,0:T(8,128)(2,1)} %param.11) | copy-start | bytes 393220
  0.6 23.4 %collective-permute-start.1 = (bf16[128,512]{1,0:T(8,128)(2,1)}, bf16[128,512]{1,0:T(8,128)(2,1)S(1)}, u32[]{:S(2)}, u32[]{:S(2)}) collective-permute-start(bf16[128,512]{1,0:T(8,128)(2,1)} %param.11), channel_id=1, source_target_pairs={{0,2},{1,3},{2,0},{3,1},{4,6},{5,7},{6,4},{7,5},{8,10},{9,11},{10,... | collective-permute-start | bytes 393224 | tf_op jit(solution)/shard_map/ppermute | solution.py:20
  7.9 14.0 %collective-permute-start = (bf16[128,512]{1,0:T(8,128)(2,1)}, bf16[128,512]{1,0:T(8,128)(2,1)S(1)}, u32[]{:S(2)}, u32[]{:S(2)}) collective-permute-start(bf16[128,512]{1,0:T(8,128)(2,1)} %param.11), channel_id=1, source_target_pairs={{0,3},{1,0},{2,1},{3,2},{4,7},{5,4},{6,5},{7,6},{8,11},{9,8},{10,9... | collective-permute-start | bytes 393224 | tf_op jit(solution)/shard_map/ppermute | solution.py:20
  7.9 16.2 %collective-permute-start.2 = (bf16[128,512]{1,0:T(8,128)(2,1)}, bf16[128,512]{1,0:T(8,128)(2,1)S(1)}, u32[]{:S(2)}, u32[]{:S(2)}) collective-permute-start(bf16[128,512]{1,0:T(8,128)(2,1)} %param.11), channel_id=1, source_target_pairs={{0,1},{1,2},{2,3},{3,0},{4,5},{5,6},{6,7},{7,4},{8,9},{9,10},{10,1... | collective-permute-start | bytes 393224 | tf_op jit(solution)/shard_map/ppermute | solution.py:20
  10.8 29.9 %collective-permute-start.7 = (bf16[336,512]{1,0:T(8,128)(2,1)}, bf16[336,512]{1,0:T(8,128)(2,1)S(1)}, u32[]{:S(2)}, u32[]{:S(2)}) collective-permute-start(bf16[336,512]{1,0:T(8,128)(2,1)} %param.10), channel_id=1, source_target_pairs={{0,4},{4,8},{8,12},{12,0},{1,5},{5,9},{9,13},{13,1},{2,6},{6,10},{... | collective-permute-start | bytes 1032200 | tf_op jit(solution)/shard_map/ppermute | solution.py:20
  12.4 28.3 %collective-permute-start.9 = (bf16[336,512]{1,0:T(8,128)(2,1)}, bf16[336,512]{1,0:T(8,128)(2,1)S(1)}, u32[]{:S(2)}, u32[]{:S(2)}) collective-permute-start(bf16[336,512]{1,0:T(8,128)(2,1)} %param.10), channel_id=1, source_target_pairs={{0,12},{4,0},{8,4},{12,8},{1,13},{5,1},{9,5},{13,9},{2,14},{6,2},{... | collective-permute-start | bytes 1032200 | tf_op jit(solution)/shard_map/ppermute | solution.py:20
  14.2 15.6 %all-to-all-start = ((s32[16,1,128]{2,1,0:T(1,128)}), s32[16,1,128]{2,1,0:T(1,128)S(1)}, u32[]{:S(2)}, u32[]{:S(2)}) async-start(s32[16,1,128]{2,1,0:T(1,128)} %broadcast_in_dim.52), calls=%async_computation | async-start | bytes 16384 | tf_op jit(solution)/shard_map/all_to_all | solution.py:24
  21.9 12.1 %copy-start.1 = (f32[5376]{0:T(1024)}, f32[5376]{0:T(1024)S(1)}, u32[]{:S(2)}) copy-start(f32[5376]{0:T(1024)S(1)} %convert_element_type.122) | copy-start | bytes 64516
  21.9 18.8 %collective-permute-start.8 = (bf16[336,512]{1,0:T(8,128)(2,1)}, bf16[336,512]{1,0:T(8,128)(2,1)}, u32[]{:S(2)}, u32[]{:S(2)}) collective-permute-start(bf16[336,512]{1,0:T(8,128)(2,1)} %param.10), channel_id=1, source_target_pairs={{0,8},{4,12},{8,0},{12,4},{1,9},{5,13},{9,1},{13,5},{2,10},{6,14},... | collective-permute-start | bytes 1032200 | tf_op jit(solution)/shard_map/ppermute | solution.py:20
  34.2 6.5 %copy-start.8 = (bf16[336,512]{1,0:T(8,128)(2,1)S(1)}, bf16[336,512]{1,0:T(8,128)(2,1)}, u32[]{:S(2)}) copy-start(bf16[336,512]{1,0:T(8,128)(2,1)} %param.10) | copy-start | bytes 1032196
  35.9 16.0 %all-to-all-start.1 = ((bf16[16,32,336]{2,1,0:T(8,128)(2,1)}), bf16[16,32,336]{2,1,0:T(8,128)(2,1)S(1)}, u32[]{:S(2)}, u32[]{:S(2)}) async-start(bf16[16,32,336]{2,1,0:T(8,128)(2,1)} %bitcast.9), calls=%async_computation.1 | async-start | bytes 786432 | tf_op jit(solution)/shard_map/all_to_all | solution.py:24
  42.7 1.4 copy-start.7
  42.7 10.7 %copy-start.6 = (bf16[336,512]{1,0:T(8,128)(2,1)}, bf16[336,512]{1,0:T(8,128)(2,1)S(1)}, u32[]{:S(2)}) copy-start(bf16[336,512]{1,0:T(8,128)(2,1)S(1)} %get-tuple-element.15) | copy-start | bytes 1032196
  42.7 16.1 %copy-start.3 = (bf16[336,512]{1,0:T(8,128)(2,1)}, bf16[336,512]{1,0:T(8,128)(2,1)S(1)}, u32[]{:S(2)}) copy-start(bf16[336,512]{1,0:T(8,128)(2,1)S(1)} %get-tuple-element.14) | copy-start | bytes 1032196
  44.1 14.6 %collective-permute-start.14 = (bf16[672,512]{1,0:T(8,128)(2,1)}, bf16[672,512]{1,0:T(8,128)(2,1)}, u32[]{:S(2)}, u32[]{:S(2)}) collective-permute-start(bf16[672,512]{1,0:T(8,128)(2,1)} %convolution_convert_fusion.3), channel_id=1, source_target_pairs={{0,16},{16,0},{1,17},{17,1},{2,18},{18,2},{3,19},{19,3},{4,20},{20... | collective-permute-start | bytes 2064392 | tf_op jit(solution)/shard_map/ppermute | solution.py:20
  53.4 14.6 %all-to-all-start.2 = ((bf16[16,32,336]{2,1,0:T(8,128)(2,1)}), bf16[16,32,336]{2,1,0:T(8,128)(2,1)S(1)}, u32[]{:S(2)}, u32[]{:S(2)}) async-start(bf16[16,32,336]{2,1,0:T(8,128)(2,1)} %reshape.158), calls=%async_computation.2 | async-start | bytes 786432 | tf_op jit(solution)/shard_map/all_to_all | solution.py:24
  69.5 5.5 %collective-permute-start.3 = (bf16[336,128]{1,0:T(8,128)(2,1)S(1)}, bf16[336,128]{1,0:T(8,128)(2,1)S(1)}, u32[]{:S(2)}, u32[]{:S(2)}) collective-permute-start(bf16[336,128]{1,0:T(8,128)(2,1)S(1)} %convolution_convert_fusion.5), channel_id=1, source_target_pairs={{0,32},{32,0},{1,33},{33,1},{2,34},{34,2},{3,35},{35,3},{4,36},{36... | collective-permute-start | bytes 258056 | tf_op jit(solution)/shard_map/ppermute | solution.py:20
  71.5 15.0 %collective-permute-start.17 = (bf16[672,128]{1,0:T(8,128)(2,1)S(1)}, bf16[672,128]{1,0:T(8,128)(2,1)S(1)}, u32[]{:S(2)}, u32[]{:S(2)}) collective-permute-start(bf16[672,128]{1,0:T(8,128)(2,1)S(1)} %bitcast.127), channel_id=1, source_target_pairs={{0,64},{64,128},{128,192},{192,0},{1,65},{65,129},{129,193},{193,1... | collective-permute-start | bytes 516104 | tf_op jit(solution)/shard_map/ppermute | solution.py:20
  71.7 14.7 %collective-permute-start.15 = (bf16[672,128]{1,0:T(8,128)(2,1)S(1)}, bf16[672,128]{1,0:T(8,128)(2,1)S(1)}, u32[]{:S(2)}, u32[]{:S(2)}) collective-permute-start(bf16[672,128]{1,0:T(8,128)(2,1)S(1)} %bitcast.126), channel_id=1, source_target_pairs={{0,192},{64,0},{128,64},{192,128},{1,193},{65,1},{129,65},{193,129... | collective-permute-start | bytes 516104 | tf_op jit(solution)/shard_map/ppermute | solution.py:20
  75.0 11.5 %collective-permute-start.16 = (bf16[672,128]{1,0:T(8,128)(2,1)S(1)}, bf16[672,128]{1,0:T(8,128)(2,1)S(1)}, u32[]{:S(2)}, u32[]{:S(2)}) collective-permute-start(bf16[672,128]{1,0:T(8,128)(2,1)S(1)} %bitcast.125), channel_id=1, source_target_pairs={{0,128},{64,192},{128,0},{192,64},{1,129},{65,193},{129,1},{193,65... | collective-permute-start | bytes 516104 | tf_op jit(solution)/shard_map/ppermute | solution.py:20
  75.0 23.3 %copy-start.9 = (bf16[336,128]{1,0:T(8,128)(2,1)}, bf16[336,128]{1,0:T(8,128)(2,1)S(1)}, u32[]{:S(2)}) copy-start(bf16[336,128]{1,0:T(8,128)(2,1)S(1)} %collective-permute-done.3) | copy-start | bytes 258052
  75.0 14.4 %collective-permute-start.6 = (bf16[672,128]{1,0:T(8,128)(2,1)S(1)}, bf16[672,128]{1,0:T(8,128)(2,1)S(1)}, u32[]{:S(2)}, u32[]{:S(2)}) collective-permute-start(bf16[672,128]{1,0:T(8,128)(2,1)S(1)} %pad_maximum_fusion.11), channel_id=1, source_target_pairs={{0,192},{64,0},{128,64},{192,128},{1,193},{65,1},{129,65},{193,129... | collective-permute-start | bytes 516104 | tf_op jit(solution)/shard_map/ppermute | solution.py:20
  76.6 12.8 %collective-permute-start.5 = (bf16[672,128]{1,0:T(8,128)(2,1)S(1)}, bf16[672,128]{1,0:T(8,128)(2,1)S(1)}, u32[]{:S(2)}, u32[]{:S(2)}) collective-permute-start(bf16[672,128]{1,0:T(8,128)(2,1)S(1)} %pad_maximum_fusion.11), channel_id=1, source_target_pairs={{0,128},{64,192},{128,0},{192,64},{1,129},{65,193},{129,1},{193,65... | collective-permute-start | bytes 516104 | tf_op jit(solution)/shard_map/ppermute | solution.py:20
  86.5 6.6 %collective-permute-start.4 = (bf16[672,128]{1,0:T(8,128)(2,1)S(1)}, bf16[672,128]{1,0:T(8,128)(2,1)S(1)}, u32[]{:S(2)}, u32[]{:S(2)}) collective-permute-start(bf16[672,128]{1,0:T(8,128)(2,1)S(1)} %pad_maximum_fusion.11), channel_id=1, source_target_pairs={{0,64},{64,128},{128,192},{192,0},{1,65},{65,129},{129,193},{193,1... | collective-permute-start | bytes 516104 | tf_op jit(solution)/shard_map/ppermute | solution.py:20
  86.6 6.7 %collective-permute-start.18 = (bf16[336,128]{1,0:T(8,128)(2,1)S(1)}, bf16[336,128]{1,0:T(8,128)(2,1)S(1)}, u32[]{:S(2)}, u32[]{:S(2)}) collective-permute-start(bf16[336,128]{1,0:T(8,128)(2,1)S(1)} %slice.41), channel_id=1, source_target_pairs={{0,32},{32,0},{1,33},{33,1},{2,34},{34,2},{3,35},{35,3},{4,36},{36... | collective-permute-start | bytes 258056 | tf_op jit(solution)/shard_map/ppermute | solution.py:20
  89.4 8.9 %copy-start.11 = (bf16[672,128]{1,0:T(8,128)(2,1)}, bf16[672,128]{1,0:T(8,128)(2,1)S(1)}, u32[]{:S(2)}) copy-start(bf16[672,128]{1,0:T(8,128)(2,1)S(1)} %collective-permute-done.6) | copy-start | bytes 516100
  89.4 5.1 %copy-start.13 = (bf16[672,128]{1,0:T(8,128)(2,1)}, bf16[672,128]{1,0:T(8,128)(2,1)S(1)}, u32[]{:S(2)}) copy-start(bf16[672,128]{1,0:T(8,128)(2,1)S(1)} %collective-permute-done.5) | copy-start | bytes 516100
  93.1 1.4 copy-start.15
  93.2 21.2 %collective-permute-start.10 = (bf16[672,512]{1,0:T(8,128)(2,1)S(1)}, bf16[672,512]{1,0:T(8,128)(2,1)}, u32[]{:S(2)}, u32[]{:S(2)}) collective-permute-start(bf16[672,512]{1,0:T(8,128)(2,1)S(1)} %pad_maximum_fusion.2), channel_id=1, source_target_pairs={{0,16},{16,0},{1,17},{17,1},{2,18},{18,2},{3,19},{19,3},{4,20},{20... | collective-permute-start | bytes 2064392 | tf_op jit(solution)/shard_map/ppermute | solution.py:20
  94.5 13.0 %all-to-all-start.3 = ((bf16[16,32,336]{2,1,0:T(8,128)(2,1)}), bf16[16,32,336]{2,1,0:T(8,128)(2,1)S(1)}, u32[]{:S(2)}, u32[]{:S(2)}) async-start(bf16[16,32,336]{2,1,0:T(8,128)(2,1)} %bitcast.36), calls=%async_computation.3 | async-start | bytes 786432 | tf_op jit(solution)/shard_map/all_to_all | solution.py:24
  108.5 31.7 %all-to-all-start.4 = ((bf16[16,32,336]{2,1,0:T(8,128)(2,1)}), bf16[16,32,336]{2,1,0:T(8,128)(2,1)S(1)}, u32[]{:S(2)}, u32[]{:S(2)}) async-start(bf16[16,32,336]{2,1,0:T(8,128)(2,1)} %copy.44), calls=%async_computation.4 | async-start | bytes 786432 | tf_op jit(solution)/shard_map/all_to_all | solution.py:24
  114.4 2.1 %copy-start.4 = (bf16[336,512]{1,0:T(8,128)(2,1)S(1)}, bf16[336,512]{1,0:T(8,128)(2,1)}, u32[]{:S(2)}) copy-start(bf16[336,512]{1,0:T(8,128)(2,1)} %copy-done.3) | copy-start | bytes 1032196
  114.4 2.1 %copy-start.5 = (bf16[336,512]{1,0:T(8,128)(2,1)S(1)}, bf16[336,512]{1,0:T(8,128)(2,1)}, u32[]{:S(2)}) copy-start(bf16[336,512]{1,0:T(8,128)(2,1)} %get-tuple-element.17) | copy-start | bytes 1032196
  114.4 2.1 %copy-start.10 = (bf16[336,128]{1,0:T(8,128)(2,1)S(1)}, bf16[336,128]{1,0:T(8,128)(2,1)}, u32[]{:S(2)}) copy-start(bf16[336,128]{1,0:T(8,128)(2,1)} %copy-done.9) | copy-start | bytes 258052
  114.4 2.1 %copy-start.12 = (bf16[672,128]{1,0:T(8,128)(2,1)S(1)}, bf16[672,128]{1,0:T(8,128)(2,1)}, u32[]{:S(2)}) copy-start(bf16[672,128]{1,0:T(8,128)(2,1)} %copy-done.11) | copy-start | bytes 516100
  114.4 2.1 %copy-start.14 = (bf16[672,128]{1,0:T(8,128)(2,1)S(1)}, bf16[672,128]{1,0:T(8,128)(2,1)}, u32[]{:S(2)}) copy-start(bf16[672,128]{1,0:T(8,128)(2,1)} %copy-done.13) | copy-start | bytes 516100
  114.4 2.1 %copy-start.16 = (bf16[672,128]{1,0:T(8,128)(2,1)S(1)}, bf16[672,128]{1,0:T(8,128)(2,1)}, u32[]{:S(2)}) copy-start(bf16[672,128]{1,0:T(8,128)(2,1)} %copy-done.15) | copy-start | bytes 516100
  117.1 14.4 %collective-permute-start.11 = (bf16[128,512]{1,0:T(8,128)(2,1)S(1)}, bf16[128,512]{1,0:T(8,128)(2,1)S(1)}, u32[]{:S(2)}, u32[]{:S(2)}) collective-permute-start(bf16[128,512]{1,0:T(8,128)(2,1)S(1)} %get-tuple-element.22), channel_id=1, source_target_pairs={{0,1},{1,2},{2,3},{3,0},{4,5},{5,6},{6,7},{7,4},{8,9},{9,10},{10,1... | collective-permute-start | bytes 393224 | tf_op jit(solution)/shard_map/ppermute | solution.py:20
  119.6 17.2 %collective-permute-start.13 = (bf16[128,512]{1,0:T(8,128)(2,1)S(1)}, bf16[128,512]{1,0:T(8,128)(2,1)S(1)}, u32[]{:S(2)}, u32[]{:S(2)}) collective-permute-start(bf16[128,512]{1,0:T(8,128)(2,1)S(1)} %get-tuple-element.23), channel_id=1, source_target_pairs={{0,3},{1,0},{2,1},{3,2},{4,7},{5,4},{6,5},{7,6},{8,11},{9,8},{10,9... | collective-permute-start | bytes 393224 | tf_op jit(solution)/shard_map/ppermute | solution.py:20
  121.4 18.2 %collective-permute-start.12 = (bf16[128,512]{1,0:T(8,128)(2,1)S(1)}, bf16[128,512]{1,0:T(8,128)(2,1)S(1)}, u32[]{:S(2)}, u32[]{:S(2)}) collective-permute-start(bf16[128,512]{1,0:T(8,128)(2,1)S(1)} %get-tuple-element.24), channel_id=1, source_target_pairs={{0,2},{1,3},{2,0},{3,1},{4,6},{5,7},{6,4},{7,5},{8,10},{9,11},{10,... | collective-permute-start | bytes 393224 | tf_op jit(solution)/shard_map/ppermute | solution.py:20
  129.5 17.2 %collective-permute-start.19 = (bf16[336,512]{1,0:T(8,128)(2,1)}, bf16[336,512]{1,0:T(8,128)(2,1)}, u32[]{:S(2)}, u32[]{:S(2)}) collective-permute-start(bf16[336,512]{1,0:T(8,128)(2,1)} %get-tuple-element.11), channel_id=1, source_target_pairs={{0,4},{4,8},{8,12},{12,0},{1,5},{5,9},{9,13},{13,1},{2,6},{6,10},{... | collective-permute-start | bytes 1032200 | tf_op jit(solution)/shard_map/ppermute | solution.py:20
  131.0 15.7 %collective-permute-start.21 = (bf16[336,512]{1,0:T(8,128)(2,1)}, bf16[336,512]{1,0:T(8,128)(2,1)}, u32[]{:S(2)}, u32[]{:S(2)}) collective-permute-start(bf16[336,512]{1,0:T(8,128)(2,1)} %get-tuple-element.12), channel_id=1, source_target_pairs={{0,12},{4,0},{8,4},{12,8},{1,13},{5,1},{9,5},{13,9},{2,14},{6,2},{... | collective-permute-start | bytes 1032200 | tf_op jit(solution)/shard_map/ppermute | solution.py:20
  131.5 15.7 %collective-permute-start.20 = (bf16[336,512]{1,0:T(8,128)(2,1)}, bf16[336,512]{1,0:T(8,128)(2,1)}, u32[]{:S(2)}, u32[]{:S(2)}) collective-permute-start(bf16[336,512]{1,0:T(8,128)(2,1)} %get-tuple-element.13), channel_id=1, source_target_pairs={{0,8},{4,12},{8,0},{12,4},{1,9},{5,13},{9,1},{13,5},{2,10},{6,14},... | collective-permute-start | bytes 1032200 | tf_op jit(solution)/shard_map/ppermute | solution.py:20
  141.5 1.1 copy-start.2

commit v3 on v2

v3 whole, which is shorter than its diff:
```python
import functools

import jax
import jax.numpy as jnp
from jax import lax
from jax.experimental import pallas as pl
from jax.experimental.pallas import tpu as pltpu
from jax.sharding import Mesh, PartitionSpec as P

EPS = 1e-06
SECTION = ("x", "z_lo", "core")
SEQ = ("y", "z_hi")
CAP = 2
BF16 = jnp.bfloat16
F32 = jnp.float32
I32 = jnp.int32
VMEM_LIMIT = 40 * 1024 * 1024
VMEM_WHOLE = 60 * 1024 * 1024

NX, NZL, NC, NY, NZH = 4, 2, 2, 4, 4
N_SECTION, N_SEQ = NX * NZL * NC, NY * NZH
NB, NF = NX, NZL * NC
BLOCK_SLOTS = N_SEQ * CAP
SLOTS = N_SECTION * BLOCK_SLOTS
GROUP = NB * CAP


def dot(a, b, contract):
    return lax.dot_general(a, b, (contract, ((), ())), preferred_element_type=F32)


def shift(x, axis, by):
    size = lax.axis_size(axis)
    return lax.ppermute(x, axis, [(i, (i + by) % size) for i in range(size)])


def swap(x, axis, k):
    return lax.ppermute(x, axis, [(i, i ^ k) for i in range(lax.axis_size(axis))])


def exchange(x, axes):
    return lax.all_to_all(x, axes, split_axis=0, concat_axis=0, tiled=True)


def call(kernel, out_shape, args, flops, scalars=1, scratch=(), after=(), in_hbm=0):
    specs = [pl.BlockSpec(memory_space=pltpu.SMEM)] * scalars
    specs += [pl.BlockSpec(memory_space=pltpu.VMEM)] * (len(args) - scalars - in_hbm)
    specs += [pl.BlockSpec(memory_space=pltpu.HBM)] * in_hbm
    leaves = jax.tree.leaves(out_shape)
    moved = sum(a.size * a.dtype.itemsize for a in list(args) + leaves)
    if after:
        specs = [pl.BlockSpec(memory_space=pl.ANY)] * len(after) + specs
        args, inner = (*after, *args), kernel

        def kernel(*refs):
            inner(*refs[len(after) :])

    return pl.pallas_call(
        kernel,
        out_shape=out_shape,
        in_specs=specs,
        out_specs=jax.tree.map(lambda _: pl.BlockSpec(memory_space=pltpu.VMEM), out_shape),
        scratch_shapes=scratch,
        compiler_params=pltpu.CompilerParams(
            vmem_limit_bytes=VMEM_WHOLE if in_hbm else VMEM_LIMIT
        ),
        cost_estimate=pl.CostEstimate(flops=flops, bytes_accessed=moved, transcendentals=0),
    )(*args)


def iota(shape, dim):
    return lax.broadcasted_iota(I32, shape, dim)


def rows_kernel(place_ref, ids_ref, gain_ref, table_ref, out_ref, rows_ref, wanted_ref, held, table, embedded, arrived):
    vocab_rows, width = table_ref.shape
    feat = out_ref.shape[-1]
    pieces = arrived.shape[0]
    columns = width // pieces
    copies = [
        pltpu.make_async_copy(
            table_ref.at[:, i * columns : (i + 1) * columns], table.at[i], arrived.at[i]
        )
        for i in range(pieces)
    ]
    for copy in copies:
        copy.start()
    n_rows, tok = N_SEQ * CAP, ids_ref.shape[1]
    which = iota((n_rows, tok), 0)
    ids = jnp.zeros((n_rows, tok), I32)
    for j in range(N_SEQ):
        ids = jnp.where(which // CAP == j, jnp.broadcast_to(ids_ref[j : j + 1, :], ids.shape), ids)
    mine = ids // vocab_rows == place_ref[0]
    token = iota((n_rows, tok), 1)
    first = jnp.min(jnp.where(mine, token, tok), axis=1, keepdims=True)
    last = jnp.max(jnp.where(mine, token, -1), axis=1, keepdims=True)
    second = which[:, :1] % CAP == 1
    chosen = jnp.where(second, last, first)
    row = jnp.sum(jnp.where(token == chosen, ids % vocab_rows, 0), axis=1, keepdims=True)
    there = jnp.logical_and(last >= 0, jnp.logical_or(jnp.logical_not(second), last != first))
    wanted = jnp.where(there, row, -1)
    wanted_ref[...] = jnp.broadcast_to(wanted, wanted_ref.shape)
    chooser = jnp.where(iota((n_rows, vocab_rows), 1) == wanted, 1.0, 0.0).astype(BF16)
    squares = jnp.zeros((n_rows, 1), F32)
    for i, copy in enumerate(copies):
        copy.wait()
        part = dot(chooser, table[i], ((1,), (0,)))
        embedded[:, i * columns : (i + 1) * columns] = part
        squares += jnp.sum(part * part, axis=1, keepdims=True)
    rows_ref[...] = embedded[...].astype(BF16)
    inv_rms = lax.rsqrt(squares / width + EPS)
    normed = (embedded[...] * inv_rms) * gain_ref[...].astype(F32)
    for f in range(NF):
        for z in range(NZH):
            start = (f * NZH + z) * feat
            low = start // 128 * 128
            high = min(-(-(start + feat) // 128) * 128, width)
            part = normed[:, low:high]
            if start != low:
                part = pltpu.roll(part, (high - low) - (start - low), 1)
            for y in range(NY):
                held[y * NZH + z, f * GROUP : (f + 1) * GROUP, :] = part[
                    y * GROUP : (y + 1) * GROUP, :feat
                ]
    out_ref[...] = held[...].astype(BF16)


def upstream_kernel(place_ref, *refs):
    cots, ws, (keep_ref, send_ref) = refs[:2], refs[2 : 2 + NY], refs[2 + NY :]
    ih, iy, core = place_ref[0], place_ref[1], place_ref[2]
    half = cots[0].shape[1] // NC

    def tokens(c):
        at = pl.ds(pl.multiple_of(c * half, half), half)
        return jnp.concatenate([cots[k // 2][k % 2, at, :] for k in range(NZH)], axis=0)

    keep, send = tokens(core), tokens(1 - core)
    for d, w in enumerate(ws):
        f = (iy - d + NY) % NY
        for tokens_of, ref in ((send, send_ref), (keep, keep_ref)):
            part = dot(tokens_of, w[...], ((1,), (1,))).astype(ref.dtype)
            for k in range(NZH):
                ref[f, ih ^ k] = part[k * half : (k + 1) * half]


def to_section_kernel(got_ref, keep_ref, recv_ref, out_ref):
    feat = got_ref.shape[-1]
    to, of = iota((SLOTS, SLOTS), 0), iota((SLOTS, SLOTS), 1)
    b, f, v, r = to // 128, to // 32 % 4, to // 2 % 16, to % 2
    order = jnp.where(of == v * 32 + f * 8 + b * 2 + r, 1.0, 0.0).astype(BF16)
    rows = dot(order, got_ref[...].reshape(SLOTS, feat), ((1,), (0,))).astype(BF16)
    out_ref[:, :BLOCK_SLOTS, :] = rows.reshape(N_SECTION, BLOCK_SLOTS, feat)
    for b in range(NB):
        for f in range(NF):
            total = keep_ref[f, b] + recv_ref[f, b].astype(F32)
            out_ref[b * NF + f, BLOCK_SLOTS:, :] = total.astype(BF16)


def at_block_kernel(ids_ref, both_ref, out_ref, *, vocab_rows):
    feat = both_ref.shape[-1]
    tok = ids_ref.shape[1]
    half = tok // NC
    up = []
    for c in range(NC):
        total = both_ref[c, BLOCK_SLOTS:, :].astype(F32)
        for i in range(1, NX * NZL):
            total += both_ref[i * NC + c, BLOCK_SLOTS:, :].astype(F32)
        up.append(total)
    up = jnp.concatenate(up, axis=0).astype(BF16)
    shard_row = jnp.broadcast_to(ids_ref[...] // vocab_rows, (tok, tok))
    down, along = iota((tok, tok), 0), iota((tok, tok), 1)
    shard_col = jnp.sum(jnp.where(down == along, shard_row, 0), axis=1, keepdims=True)
    same = shard_row == shard_col
    rank_col = jnp.sum(jnp.where(jnp.logical_and(same, along < down), 1, 0), axis=1, keepdims=True)
    rank_row = jnp.sum(jnp.where(jnp.logical_and(same, down < along), 1, 0), axis=0, keepdims=True)
    slot_col = shard_col * CAP + rank_col
    slot_row = ids_ref[...] // vocab_rows * CAP + rank_row
    place = jnp.where(iota((tok, SLOTS), 1) == slot_col, 1.0, 0.0).astype(BF16)
    place_back = jnp.where(iota((SLOTS, tok), 0) == slot_row, 1.0, 0.0).astype(BF16)
    got = both_ref[:, :BLOCK_SLOTS, :].reshape(SLOTS, feat)
    normed = dot(place, got, ((1,), (0,))).astype(BF16)
    back = dot(place_back, up, ((1,), (0,))).astype(BF16)
    out_ref[:, :BLOCK_SLOTS, :] = back.reshape(N_SECTION, BLOCK_SLOTS, feat)
    for s in range(N_SECTION):
        c = s % NC
        out_ref[s, BLOCK_SLOTS:, :] = normed[c * half : (c + 1) * half]


def to_seq_kernel(both_ref, out_ref):
    feat = both_ref.shape[-1]
    to, of = iota((SLOTS, SLOTS), 0), iota((SLOTS, SLOTS), 1)
    v, f, b, r = to // 32, to // 8 % 4, to // 2 % 4, to % 2
    order = jnp.where(of == b * 128 + f * 32 + v * 2 + r, 1.0, 0.0).astype(BF16)
    rows = both_ref[:, :BLOCK_SLOTS, :].reshape(SLOTS, feat)
    rows = dot(order, rows, ((1,), (0,))).astype(BF16)
    out_ref[...] = rows.reshape(N_SEQ, BLOCK_SLOTS, feat)


def products_kernel(place_ref, own_ref, other_ref, *refs):
    sources, refs = refs[: 2 + NY], refs[2 + NY :]
    projs, grads = refs[:NZH], refs[NZH : NZH + NY]
    cots, ws, arrived = refs[NZH + NY :]
    targets = [cots.at[:2], cots.at[2:]] + [ws.at[d] for d in range(NY)]
    copies = [
        pltpu.make_async_copy(source, target, arrived.at[i])
        for i, (source, target) in enumerate(zip(sources, targets))
    ]
    for copy in copies:
        copy.start()
    ih, iy, core = place_ref[0], place_ref[1], place_ref[2]
    tok = cots.shape[1]
    half = tok // NC
    at = [pl.ds(pl.multiple_of(c * half, half), half) for c in (core, 1 - core)]
    blocks = [(ih + d) % NZH for d in range(NZH)]
    copies[0].wait()
    copies[1].wait()
    cot = jnp.concatenate([cots[b ^ ih, a, :] for b in blocks for a in at], axis=0)
    proj = None
    for d in range(NY):
        f = (iy + d) % NY
        parts = []
        for b in blocks:
            parts += [ref[b * NF + f, BLOCK_SLOTS:, :] for ref in (own_ref, other_ref)]
        normed = jnp.concatenate(parts, axis=0)
        grads[d][...] = dot(normed, cot, ((0,), (0,))).astype(BF16)
        copies[2 + -d % NY].wait()
        term = dot(normed, ws[-d % NY], ((1,), (0,)))
        proj = term if proj is None else proj + term
    for d in range(NZH):
        for c, a in enumerate(at):
            first = (d * NC + c) * half
            projs[d][a, :] = proj[first : first + half].astype(BF16)


def table_kernel(back_ref, rows_ref, gain_ref, wanted_ref, *refs):
    out_ref, gathered, padded, grads = refs[-4:]
    feat = back_ref.shape[-1]
    n_rows, width = rows_ref.shape
    step, columns = pl.program_id(0), out_ref.shape[1]

    @pl.when(step == 0)
    def _():
        gathered[...] = jnp.zeros_like(gathered)
        padded[...] = jnp.zeros_like(padded)
        for y in range(NY):
            for z in range(NZH):
                part = back_ref[y * NZH + z].astype(F32)
                for f in range(NF):
                    padded[f * NZH + z, y * GROUP : (y + 1) * GROUP, :feat] = part[
                        f * GROUP : (f + 1) * GROUP
                    ]
        for i in range(NF * NZH):
            start = i * feat
            low = start // 128 * 128
            high = min(-(-(start + feat) // 128) * 128, width)
            part = padded[i, :, : high - low]
            if start != low:
                part = pltpu.roll(part, start - low, 1)
            gathered[:, low:high] += part
        embedded = rows_ref[...].astype(F32)
        inv_rms = lax.rsqrt(jnp.mean(embedded * embedded, axis=1, keepdims=True) + EPS)
        unit_rows = embedded * inv_rms
        scaled = gathered[...] * gain_ref[...].astype(F32)
        inner = jnp.mean(scaled * unit_rows, axis=1, keepdims=True)
        result = (inv_rms * (scaled - unit_rows * inner)).astype(BF16)
        for i in range(width // columns):
            grads[i] = result[:, i * columns : (i + 1) * columns]

    chooser = jnp.where(iota((n_rows, out_ref.shape[0]), 1) == wanted_ref[:, :1], 1.0, 0.0)
    out_ref[...] = dot(chooser.astype(BF16), grads[step], ((0,), (0,))).astype(BF16)


def table_call(back, rows, gain, wanted, vocab_rows, after):
    n_rows, width = rows.shape
    feat = back.shape[-1]
    steps = 6
    columns = width // steps
    args = (back, rows, gain, wanted)
    return pl.pallas_call(
        table_kernel,
        grid=(steps,),
        out_shape=jax.ShapeDtypeStruct((vocab_rows, width), BF16),
        in_specs=[pl.BlockSpec(a.shape, lambda i, n=a.ndim: (0,) * n) for a in args]
        + [pl.BlockSpec(memory_space=pl.ANY)] * len(after),
        out_specs=pl.BlockSpec((vocab_rows, columns), lambda i: (0, i)),
        scratch_shapes=[
            pltpu.VMEM((n_rows, width), F32),
            pltpu.VMEM((NF * NZH, n_rows, -(-feat // 128) * 128 + 128), F32),
            pltpu.VMEM((steps, n_rows, columns), BF16),
        ],
        compiler_params=pltpu.CompilerParams(vmem_limit_bytes=VMEM_LIMIT),
        cost_estimate=pl.CostEstimate(
            flops=2 * vocab_rows * n_rows * width, bytes_accessed=2 * vocab_rows * width,
            transcendentals=0,
        ),
    )(*args, *after)


def sum_f32(parts):
    total = parts[0].astype(F32)
    for part in parts[1:]:
        total = total + part.astype(F32)
    return total


def per_device(embed_table, vocab_shard, shard_row, norm_gain, weight, cotangent):
    vocab_rows, model_width = embed_table.shape
    tok = shard_row.shape[0]
    feat, cols = weight.shape
    half = tok // NC
    section, seq = lax.axis_index(SECTION), lax.axis_index(SEQ)
    ix, iz, ic, iy, ih = (lax.axis_index(a) for a in SECTION + SEQ)
    where = jnp.stack([ih, iy, ic]).astype(I32)
    shape = jax.ShapeDtypeStruct

    ids = vocab_shard[:, 0] * vocab_rows + shard_row
    all_ids = exchange(jnp.broadcast_to(ids[None], (N_SEQ, tok)), SEQ)

    ws = [shift(weight, "y", d) for d in range(1, NY)]
    near = swap(cotangent, "z_hi", 1)
    gain = norm_gain.reshape(1, -1)
    all_ids, gain, near, *ws = lax.optimization_barrier((all_ids, gain, near, *ws))
    ws = [weight, *ws]
    near = jnp.stack([cotangent, near])
    cots = [near, swap(near, "z_hi", 2)]

    shard = (section * N_SEQ + seq).astype(I32).reshape(1)
    out_rows, rows, wanted = call(
        rows_kernel,
        (
            shape((N_SEQ, NF * GROUP, feat), BF16),
            shape((N_SEQ * CAP, model_width), BF16),
            shape((N_SEQ * CAP, 128), I32),
        ),
        (shard, all_ids, gain, embed_table),
        flops=2 * N_SEQ * CAP * vocab_rows * model_width,
        in_hbm=1,
        scratch=[
            pltpu.VMEM((N_SEQ, NF * GROUP, feat), F32),
            pltpu.VMEM((6, vocab_rows, model_width // 6), BF16),
            pltpu.VMEM((N_SEQ * CAP, model_width), F32),
            pltpu.SemaphoreType.DMA((6,)),
        ],
    )
    got = exchange(out_rows, SEQ)

    keep, send = call(
        upstream_kernel,
        (shape((NF, NB, half, feat), F32), shape((NF, NB, half, feat), BF16)),
        (where, *cots, *ws),
        flops=2 * NB * tok * NF * feat * cols,
        after=(wanted,),
    )
    recv = jnp.concatenate([swap(send[i : i + 1], "core", 1) for i in range(NF)], axis=0)

    width = BLOCK_SLOTS + half
    both = call(
        to_section_kernel, shape((N_SECTION, width, feat), BF16), (got, keep, recv),
        flops=2 * SLOTS * SLOTS * feat, scalars=0,
    )
    both = exchange(both, SECTION)
    block_ids = lax.dynamic_slice_in_dim(all_ids, iy * NZH + ix, 1, 0)
    both = call(
        functools.partial(at_block_kernel, vocab_rows=vocab_rows),
        shape((N_SECTION, width, feat), BF16), (block_ids, both),
        flops=4 * tok * SLOTS * feat, scalars=0,
    )
    both = exchange(both, SECTION)
    back = call(
        to_seq_kernel, shape((N_SEQ, BLOCK_SLOTS, feat), BF16), (both,),
        flops=2 * SLOTS * SLOTS * feat, scalars=0,
    )
    back = exchange(back, SEQ)

    products = call(
        products_kernel,
        (shape((tok, cols), BF16),) * NZH + (shape((feat, cols), BF16),) * NY,
        (where, both, swap(both, "core", 1), *cots, *ws),
        flops=4 * NB * tok * NF * feat * cols,
        in_hbm=2 + NY,
        scratch=[
            pltpu.VMEM((NZH, tok, cols), BF16),
            pltpu.VMEM((NY, feat, cols), BF16),
            pltpu.SemaphoreType.DMA((2 + NY,)),
        ],
    )
    proj, grad = products[:NZH], products[NZH:]
    grad_parts = [shift(grad[d], "y", d) for d in range(1, NY)]
    proj_parts = [shift(proj[d], "z_hi", d) for d in range(1, NZH)]
    weight_grad = sum_f32([grad[0], *grad_parts]).astype(BF16)
    projected = sum_f32([proj[0], *proj_parts]).astype(BF16)

    table_grad = table_call(back, rows, gain, wanted, vocab_rows, after=proj_parts)
    return projected, table_grad, weight_grad


def solution(mesh):
    fine = Mesh(mesh.devices.reshape(NX, NZL, NC, NY, NZH), SECTION + SEQ)
    in_specs = (
        P(SECTION + SEQ, None),
        P(SEQ, None),
        P(SEQ),
        P(),
        P(SEQ, SECTION),
        P(SEQ, SECTION),
    )
    out_specs = (P(SEQ, SECTION), P(SECTION + SEQ, None), P(SEQ, SECTION))
    return jax.shard_map(
        per_device, mesh=fine, in_specs=in_specs, out_specs=out_specs, check_vma=False
    )
```

time: 151 us -> 145 us (0.960)
  Pallas kernels: 0 us -> 21.9 us
  blocking collectives: 0 us -> 20.6 us
  matrix products: 17.3 us -> 0 us
  starting transfers between devices: 62.7 us -> 52.2 us
  waiting for transfers between devices: 47.9 us -> 37.7 us
  local copies, waits for them, and re-layouts: 11.8 us -> 7.14 us
  other arithmetic: 7.45 us -> 3.65 us
    pallas_call x0 -> x7, Pallas kernels: none -> 21.9 us  [the longest x6 16.6 us: call(): pl.pallas_call(kernel, out_shape=out_shape, in_specs=specs, out_specs=jax...]
    all_to_all x0 -> x1, blocking collectives: none -> 20.6 us  [exchange(): return lax.all_to_all(x, axes, split_axis=0, concat_axis=0, tiled=True)]
    dot_general x10 -> x0, matrix products: 17.3 us -> none  [dot(): lax.dot_general(a, b, (contract, ((), ())), preferred_element_type=F32)]
    ppermute x22 -> x9, starting transfers between devices: 36.4 us -> 19.3 us  [shift(): return lax.ppermute(x, axis, [(i, (i + by) % size) for i in range(size)])]
    ppermute x22 -> x9, waiting for transfers between devices: 20.7 us -> 7.99 us  [shift(): return lax.ppermute(x, axis, [(i, (i + by) % size) for i in range(size)])]
    ppermute x0 -> x7, starting transfers between devices: none -> 5.07 us  [swap(): lax.ppermute(x, axis, [(i, i ^ k) for i in range(lax.axis_size(axis))])]
    unnamed x44 -> x36, local copies, waits for them, and re-layouts: 1.13 us -> 4.43 us
    reshape x8 -> x1, local copies, waits for them, and re-layouts: 4.32 us -> 1.31 us  [per_device(): gain = norm_gain.reshape(1, -1)]
  transfers between devices with their start and end apart: 27 -> 20, of which waited for: 10 -> 10; matrix products, arithmetic and copies ran while one was open for 22% -> 3% of each run, Pallas kernels for 0% -> 14%
where the time goes in v3:
time: 145 us; the launch traced here: 144 us
  starting transfers between devices  52.2 us (36%)
  waiting for transfers between devices  37.7 us (26%)
  Pallas kernels  21.9 us (15%)
  blocking collectives  20.6 us (14%)
  local copies, waits for them, and re-layouts  7.14 us (5%)
  other arithmetic  3.65 us (3%)
    all_to_all x4, waiting for transfers between devices, exchange(): return lax.all_to_all(x, axes, split_axis=0, concat_axis=0, tiled=True)  28.1 us
    all_to_all x4, starting transfers between devices, exchange(): return lax.all_to_all(x, axes, split_axis=0, concat_axis=0, tiled=True)  27.8 us
    all_to_all x1, blocking collectives, exchange(): return lax.all_to_all(x, axes, split_axis=0, concat_axis=0, tiled=True)  20.6 us
    ppermute x9, starting transfers between devices, shift(): return lax.ppermute(x, axis, [(i, (i + by) % size) for i in range(size)])  19.3 us
    pallas_call x6, Pallas kernels, call(): pl.pallas_call(kernel, out_shape=out_shape, in_specs=specs, out_specs=jax...  16.6 us
    ppermute x9, waiting for transfers between devices, shift(): return lax.ppermute(x, axis, [(i, (i + by) % size) for i in range(size)])  7.99 us
    pallas_call x1, Pallas kernels, table_call(): pl.pallas_call(table_kernel, grid=(steps,), out_shape=jax.ShapeDtypeStruc...  5.29 us
    ppermute x7, starting transfers between devices, swap(): lax.ppermute(x, axis, [(i, i ^ k) for i in range(lax.axis_size(axis))])  5.07 us
  transfers between devices with their start and end apart: 20, of which 10 were waited for; matrix products, arithmetic and copies ran while one was open for 3% of the time, Pallas kernels for 14%

profile of v3, /device:TPU:8, one launch (start us, length us, event | category | flops | bytes accessed | tf_op | source)
XLA Modules:
  0.0 144.1 jit_solution(187840275063048092)
XLA Ops:
  0.6 2.3 %collective-permute-start.3 = (bf16[336,512]{1,0:T(8,128)(2,1)}, bf16[336,512]{1,0:T(8,128)(2,1)S(1)}, u32[]{:S(2)}, u32[]{:S(2)}) collective-permute-start(bf16[336,512]{1,0:T(8,128)(2,1)} %refs_2_.1), channel_id=1, source_target_pairs={{0,12},{4,0},{8,4},{12,8},{1,13},{5,1},{9,5},{13,9},{2,14},{6,2},{... | collective-permute-start | bytes 1032200 | tf_op jit(solution)/shard_map/ppermute | solution.py:34
  2.9 0.9 collective-permute-start.2
  3.7 1.9 %collective-permute-start.1 = (bf16[336,512]{1,0:T(8,128)(2,1)}, bf16[336,512]{1,0:T(8,128)(2,1)S(1)}, u32[]{:S(2)}, u32[]{:S(2)}) collective-permute-start(bf16[336,512]{1,0:T(8,128)(2,1)} %refs_2_.1), channel_id=1, source_target_pairs={{0,4},{4,8},{8,12},{12,0},{1,5},{5,9},{9,13},{13,1},{2,6},{6,10},{... | collective-permute-start | bytes 1032200 | tf_op jit(solution)/shard_map/ppermute | solution.py:34
  5.6 3.3 %collective-permute-start = (bf16[128,512]{1,0:T(8,128)(2,1)}, bf16[128,512]{1,0:T(8,128)(2,1)S(1)}, u32[]{:S(2)}, u32[]{:S(2)}) collective-permute-start(bf16[128,512]{1,0:T(8,128)(2,1)} %param.11), channel_id=1, source_target_pairs={{0,1},{1,0},{2,3},{3,2},{4,5},{5,4},{6,7},{7,6},{8,9},{9,8},{10,11... | collective-permute-start | bytes 393224 | tf_op jit(solution)/shard_map/ppermute | solution.py:38
  8.9 0.7 bitcast_add_fusion
  9.6 0.6 broadcast_in_dim.2
  10.2 8.5 %all-to-all-start = ((s32[16,1,128]{2,1,0:T(1,128)}), s32[16,1,128]{2,1,0:T(1,128)S(1)}, u32[]{:S(2)}, u32[]{:S(2)}) async-start(s32[16,1,128]{2,1,0:T(1,128)} %broadcast_in_dim.2), calls=%async_computation | async-start | bytes 16384 | tf_op jit(solution)/shard_map/all_to_all | solution.py:42
  18.7 1.3 reshape.20.gain_ref
  20.0 7.2 %all-to-all-done = s32[16,1,128]{2,1,0:T(1,128)S(1)} async-done(((s32[16,1,128]{2,1,0:T(1,128)}), s32[16,1,128]{2,1,0:T(1,128)S(1)}, u32[]{:S(2)}, u32[]{:S(2)}) %all-to-all-start) | async-done | bytes 8224 | tf_op jit(solution)/shard_map/all_to_all | solution.py:42
  27.3 1.1 pad_maximum_fusion.1.refs_2_.refs_0_
  28.4 0.7 collective-permute-start.4
  29.1 5.3 %shard_map.85 = (bf16[16,32,336]{2,1,0:T(8,128)(2,1)}, bf16[32,5376]{1,0:T(8,128)(2,1)}, s32[32,128]{1,0:T(8,128)}) custom-call(s32[1]{0:T(128)} %bitcast.5.place_ref, s32[16,128]{1,0:T(8,128)} %bitcast.11, bf16[1,5376]{1,0:T(2,128)(2,1)} %reshape.20.gain_ref, bf16[512,5376]{1,0:T(8,128)(2,1)} %table_ref.1), custom_call_target="tpu_custom_call" | custom-call | flops 176160768 | bytes 6228484 | tf_op jit(solution)/shard_map/pallas_call | solution.py:58
  34.4 8.7 %all-to-all-start.1 = ((bf16[16,32,336]{2,1,0:T(8,128)(2,1)}), bf16[16,32,336]{2,1,0:T(8,128)(2,1)S(1)}, u32[]{:S(2)}, u32[]{:S(2)}) async-start(bf16[16,32,336]{2,1,0:T(8,128)(2,1)} %get-tuple-element.24), calls=%async_computation.1 | async-start | bytes 786432 | tf_op jit(solution)/shard_map/all_to_all | solution.py:42
  43.2 0.3 collective-permute-done.4.refs_3_.refs_1_
  43.5 0.7 copy-done.12
  44.3 0.7 copy-done.4
  45.0 1.0 copy-done.11
  46.0 0.9 copy-done.13
  46.9 1.8 %shard_map.86 = (f32[4,4,64,336]{3,2,1,0:T(8,128)S(1)}, bf16[4,4,64,336]{3,2,1,0:T(8,128)(2,1)S(1)}) custom-call(s32[32,128]{1,0:T(8,128)S(1)} %copy-done.4, s32[3]{0:T(128)S(1)} %pad_add_fusion.refs_1_.place_ref, bf16[2,128,512]{2,1,0:T(8,128)(2,1)S(1)} %pad_maximum_fusion.1.refs_2_.refs_0_, bf16[2,128,512]{2,1,0:T(8,128)(2,1)S(1)} %copy-done.13, ...), custom_call_target="tpu_custom_call" | custom-call | flops 704643072 | bytes 3964940 | tf_op jit(solution)/shard_map/pallas_call | solution.py:58
  48.9 0.5 collective-permute-start.8
  49.5 0.4 collective-permute-start.6
  49.9 0.4 collective-permute-done.5
  50.4 0.3 collective-permute-done.8
  50.6 0.3 collective-permute-done.7
  50.9 0.3 collective-permute-done.6
  51.2 0.2 pad_maximum_fusion.recv_ref
  51.4 3.6 %all-to-all-done.1.got_ref = bf16[16,32,336]{2,1,0:T(8,128)(2,1)S(1)} async-done(((bf16[16,32,336]{2,1,0:T(8,128)(2,1)}), bf16[16,32,336]{2,1,0:T(8,128)(2,1)S(1)}, u32[]{:S(2)}, u32[]{:S(2)}) %all-to-all-start.1) | async-done | bytes 344096 | tf_op jit(solution)/shard_map/all_to_all | solution.py:42
  55.0 1.5 %shard_map.87 = bf16[16,96,336]{2,1,0:T(8,128)(2,1)} custom-call(bf16[16,32,336]{2,1,0:T(8,128)(2,1)S(1)} %all-to-all-done.1.got_ref, f32[4,4,64,336]{3,2,1,0:T(8,128)S(1)} %get-tuple-element.30.keep_ref, bf16[4,4,64,336]{3,2,1,0:T(8,128)(2,1)S(1)} %pad_maximum_fusion.recv_ref), custom_call_target="tpu_custom_call" | custom-call | flops 176160768 | bytes 3440640 | tf_op jit(solution)/shard_map/pallas_call | solution.py:58
  56.5 4.5 %all-to-all-start.2 = ((bf16[16,96,336]{2,1,0:T(8,128)(2,1)}), bf16[16,96,336]{2,1,0:T(8,128)(2,1)S(1)}, u32[]{:S(2)}, u32[]{:S(2)}) async-start(bf16[16,96,336]{2,1,0:T(8,128)(2,1)} %shard_map.87), calls=%async_computation.2 | async-start | bytes 2359296 | tf_op jit(solution)/shard_map/all_to_all | solution.py:42
  61.0 0.7 constant_dynamic-slice_fusion.ids_ref
  61.7 17.4 %all-to-all-done.2.both_ref = bf16[16,96,336]{2,1,0:T(8,128)(2,1)S(1)} async-done(((bf16[16,96,336]{2,1,0:T(8,128)(2,1)}), bf16[16,96,336]{2,1,0:T(8,128)(2,1)S(1)}, u32[]{:S(2)}, u32[]{:S(2)}) %all-to-all-start.2) | async-done | bytes 1032224 | tf_op jit(solution)/shard_map/all_to_all | solution.py:42
  79.1 0.5 shard_map.88
  79.6 20.6 %all_to_all.29.own_ref.both_ref = bf16[16,96,336]{2,1,0:T(8,128)(2,1)S(1)} all-to-all(bf16[16,96,336]{2,1,0:T(8,128)(2,1)S(1)} %shard_map.88), channel_id=1, replica_groups=mesh['x'=4,'z_lo'=2,'core'=2,'y'=4,'z_hi'=4] {'x','z_lo','core'}, dimensions={0} | all-to-all | bytes 2064384 | tf_op jit(solution)/shard_map/all_to_all | solution.py:42
  100.2 1.2 shard_map.90
  101.4 6.1 %all-to-all-start.4 = ((bf16[16,32,336]{2,1,0:T(8,128)(2,1)}), bf16[16,32,336]{2,1,0:T(8,128)(2,1)S(1)}, u32[]{:S(2)}, u32[]{:S(2)}) async-start(bf16[16,32,336]{2,1,0:T(8,128)(2,1)} %shard_map.90), calls=%async_computation.4 | async-start | bytes 786432 | tf_op jit(solution)/shard_map/all_to_all | solution.py:42
  107.6 1.0 copy-done.17
  108.6 6.2 %shard_map.89 = (bf16[128,512]{1,0:T(8,128)(2,1)}, bf16[128,512]{1,0:T(8,128)(2,1)}, bf16[128,512]{1,0:T(8,128)(2,1)}, bf16[128,512]{1,0:T(8,128)(2,1)}, bf16[33...) custom-call(s32[3]{0:T(128)} %copy-done.6, ...), custom_call_target="tpu_custom_call" | custom-call | flops 1409286144 | bytes 5865484 | tf_op jit(solution)/shard_map/pallas_call | solution.py:58
  114.8 2.4 %collective-permute-start.10 = (bf16[128,512]{1,0:T(8,128)(2,1)}, bf16[128,512]{1,0:T(8,128)(2,1)S(1)}, u32[]{:S(2)}, u32[]{:S(2)}) collective-permute-start(bf16[128,512]{1,0:T(8,128)(2,1)} %get-tuple-element.33), channel_id=1, source_target_pairs={{0,1},{1,2},{2,3},{3,0},{4,5},{5,6},{6,7},{7,4},{8,9},{9,10},{10,1... | collective-permute-start | bytes 393224 | tf_op jit(solution)/shard_map/ppermute | solution.py:34
  117.3 3.6 %collective-permute-start.11 = (bf16[128,512]{1,0:T(8,128)(2,1)}, bf16[128,512]{1,0:T(8,128)(2,1)S(1)}, u32[]{:S(2)}, u32[]{:S(2)}) collective-permute-start(bf16[128,512]{1,0:T(8,128)(2,1)} %get-tuple-element.34), channel_id=1, source_target_pairs={{0,2},{1,3},{2,0},{3,1},{4,6},{5,7},{6,4},{7,5},{8,10},{9,11},{10,... | collective-permute-start | bytes 393224 | tf_op jit(solution)/shard_map/ppermute | solution.py:34
  120.8 3.6 %collective-permute-start.12 = (bf16[128,512]{1,0:T(8,128)(2,1)}, bf16[128,512]{1,0:T(8,128)(2,1)S(1)}, u32[]{:S(2)}, u32[]{:S(2)}) collective-permute-start(bf16[128,512]{1,0:T(8,128)(2,1)} %get-tuple-element.35), channel_id=1, source_target_pairs={{0,3},{1,0},{2,1},{3,2},{4,7},{5,4},{6,5},{7,6},{8,11},{9,8},{10,9... | collective-permute-start | bytes 393224 | tf_op jit(solution)/shard_map/ppermute | solution.py:34
  124.4 1.5 %collective-permute-start.13 = (bf16[336,512]{1,0:T(8,128)(2,1)}, bf16[336,512]{1,0:T(8,128)(2,1)S(1)}, u32[]{:S(2)}, u32[]{:S(2)}) collective-permute-start(bf16[336,512]{1,0:T(8,128)(2,1)} %get-tuple-element.38), channel_id=1, source_target_pairs={{0,4},{4,8},{8,12},{12,0},{1,5},{5,9},{9,13},{13,1},{2,6},{6,10},{... | collective-permute-start | bytes 1032200 | tf_op jit(solution)/shard_map/ppermute | solution.py:34
  125.9 1.2 collective-permute-start.14
  127.1 2.1 %collective-permute-start.15 = (bf16[336,512]{1,0:T(8,128)(2,1)}, bf16[336,512]{1,0:T(8,128)(2,1)S(1)}, u32[]{:S(2)}, u32[]{:S(2)}) collective-permute-start(bf16[336,512]{1,0:T(8,128)(2,1)} %get-tuple-element.40), channel_id=1, source_target_pairs={{0,12},{4,0},{8,4},{12,8},{1,13},{5,1},{9,5},{13,9},{2,14},{6,2},{... | collective-permute-start | bytes 1032200 | tf_op jit(solution)/shard_map/ppermute | solution.py:34
  129.1 4.5 %collective-permute-done.12.refs_2_ = bf16[128,512]{1,0:T(8,128)(2,1)S(1)} collective-permute-done((bf16[128,512]{1,0:T(8,128)(2,1)}, bf16[128,512]{1,0:T(8,128)(2,1)S(1)}, u32[]{:S(2)}, u32[]{:S(2)}) %collective-permute-start.12) | collective-permute-done | bytes 131104 | tf_op jit(solution)/shard_map/ppermute | solution.py:34
  133.6 5.3 %shard_map.91 = bf16[512,5376]{1,0:T(8,128)(2,1)} custom-call(bf16[16,32,336]{2,1,0:T(8,128)(2,1)S(1)} %all-to-all-done.4.back_ref, bf16[32,5376]{1,0:T(8,128)(2,1)S(1)} %copy-done.1, bf16[1,5376]{1,0:T(2,128)(2,1)S(1)} %copy-done.3, s32[32,128]{1,0:T(8,128)S(1)} %copy-done.5, bf16[128,512]{1,0:T(8,128)(2,1)S(1)} %collective-permute-done.10.refs_0_, ...), custom_call_target="tpu_custom_call" | custom-call | flops 176160768 | bytes 5505024 | tf_op jit(solution)/shard_map/pallas_call | solution.py:279
  138.9 0.7 add_convert_fusion.1
  139.6 3.5 %collective-permute-done.15 = bf16[336,512]{1,0:T(8,128)(2,1)S(1)} collective-permute-done((bf16[336,512]{1,0:T(8,128)(2,1)}, bf16[336,512]{1,0:T(8,128)(2,1)S(1)}, u32[]{:S(2)}, u32[]{:S(2)}) %collective-permute-start.15) | collective-permute-done | bytes 344096 | tf_op jit(solution)/shard_map/ppermute | solution.py:34
  143.1 0.9 add_convert_fusion
  (46 shorter events, 0.5 us)
Async XLA Ops:
  0.6 26.6 %collective-permute-start.3 = (bf16[336,512]{1,0:T(8,128)(2,1)}, bf16[336,512]{1,0:T(8,128)(2,1)S(1)}, u32[]{:S(2)}, u32[]{:S(2)}) collective-permute-start(bf16[336,512]{1,0:T(8,128)(2,1)} %refs_2_.1), channel_id=1, source_target_pairs={{0,12},{4,0},{8,4},{12,8},{1,13},{5,1},{9,5},{13,9},{2,14},{6,2},{... | collective-permute-start | bytes 1032200 | tf_op jit(solution)/shard_map/ppermute | solution.py:34
  2.9 24.4 %collective-permute-start.2 = (bf16[336,512]{1,0:T(8,128)(2,1)}, bf16[336,512]{1,0:T(8,128)(2,1)S(1)}, u32[]{:S(2)}, u32[]{:S(2)}) collective-permute-start(bf16[336,512]{1,0:T(8,128)(2,1)} %refs_2_.1), channel_id=1, source_target_pairs={{0,8},{4,12},{8,0},{12,4},{1,9},{5,13},{9,1},{13,5},{2,10},{6,14},... | collective-permute-start | bytes 1032200 | tf_op jit(solution)/shard_map/ppermute | solution.py:34
  3.7 23.5 %collective-permute-start.1 = (bf16[336,512]{1,0:T(8,128)(2,1)}, bf16[336,512]{1,0:T(8,128)(2,1)S(1)}, u32[]{:S(2)}, u32[]{:S(2)}) collective-permute-start(bf16[336,512]{1,0:T(8,128)(2,1)} %refs_2_.1), channel_id=1, source_target_pairs={{0,4},{4,8},{8,12},{12,0},{1,5},{5,9},{9,13},{13,1},{2,6},{6,10},{... | collective-permute-start | bytes 1032200 | tf_op jit(solution)/shard_map/ppermute | solution.py:34
  5.6 21.6 %collective-permute-start = (bf16[128,512]{1,0:T(8,128)(2,1)}, bf16[128,512]{1,0:T(8,128)(2,1)S(1)}, u32[]{:S(2)}, u32[]{:S(2)}) collective-permute-start(bf16[128,512]{1,0:T(8,128)(2,1)} %param.11), channel_id=1, source_target_pairs={{0,1},{1,0},{2,3},{3,2},{4,5},{5,4},{6,7},{7,6},{8,9},{9,8},{10,11... | collective-permute-start | bytes 393224 | tf_op jit(solution)/shard_map/ppermute | solution.py:38
  10.2 17.0 %all-to-all-start = ((s32[16,1,128]{2,1,0:T(1,128)}), s32[16,1,128]{2,1,0:T(1,128)S(1)}, u32[]{:S(2)}, u32[]{:S(2)}) async-start(s32[16,1,128]{2,1,0:T(1,128)} %broadcast_in_dim.2), calls=%async_computation | async-start | bytes 16384 | tf_op jit(solution)/shard_map/all_to_all | solution.py:42
  27.2 1.9 %copy-start.16 = (s32[16,1,128]{2,1,0:T(1,128)}, s32[16,1,128]{2,1,0:T(1,128)S(1)}, u32[]{:S(2)}) copy-start(s32[16,1,128]{2,1,0:T(1,128)S(1)} %all-to-all-done) | copy-start | bytes 24580
  27.2 17.0 %copy-start.8 = (bf16[336,512]{1,0:T(8,128)(2,1)}, bf16[336,512]{1,0:T(8,128)(2,1)S(1)}, u32[]{:S(2)}) copy-start(bf16[336,512]{1,0:T(8,128)(2,1)S(1)} %collective-permute-done.3.refs_7_.refs_5_) | copy-start | bytes 1032196
  27.3 17.0 %copy-start.9 = (bf16[336,512]{1,0:T(8,128)(2,1)}, bf16[336,512]{1,0:T(8,128)(2,1)S(1)}, u32[]{:S(2)}) copy-start(bf16[336,512]{1,0:T(8,128)(2,1)S(1)} %collective-permute-done.2.refs_6_.refs_4_) | copy-start | bytes 1032196
  27.3 7.2 %copy-start.10 = (bf16[336,512]{1,0:T(8,128)(2,1)}, bf16[336,512]{1,0:T(8,128)(2,1)S(1)}, u32[]{:S(2)}) copy-start(bf16[336,512]{1,0:T(8,128)(2,1)S(1)} %collective-permute-done.1.refs_5_.refs_3_) | copy-start | bytes 1032196
  28.4 15.9 %copy-start.2 = (bf16[2,128,512]{2,1,0:T(8,128)(2,1)}, bf16[2,128,512]{2,1,0:T(8,128)(2,1)S(1)}, u32[]{:S(2)}) copy-start(bf16[2,128,512]{2,1,0:T(8,128)(2,1)S(1)} %pad_maximum_fusion.1.refs_2_.refs_0_) | copy-start | bytes 786436
  28.4 15.2 %collective-permute-start.4 = (bf16[2,128,512]{2,1,0:T(8,128)(2,1)S(1)}, bf16[2,128,512]{2,1,0:T(8,128)(2,1)S(1)}, u32[]{:S(2)}, u32[]{:S(2)}) collective-permute-start(bf16[2,128,512]{2,1,0:T(8,128)(2,1)S(1)} %pad_maximum_fusion.1.refs_2_.refs_0_), channel_id=1, source_target_pairs={{0,2},{1,3},{2,0},{3,1},{4,6},{5,7},{6,4},{7,5},{8,10},{9,11},{10,... | collective-permute-start | bytes 786440 | tf_op jit(solution)/shard_map/ppermute | solution.py:38
  29.1 15.2 %copy-start.7 = (bf16[336,512]{1,0:T(8,128)(2,1)S(1)}, bf16[336,512]{1,0:T(8,128)(2,1)}, u32[]{:S(2)}) copy-start(bf16[336,512]{1,0:T(8,128)(2,1)} %refs_2_.1) | copy-start | bytes 1032196
  34.4 20.5 %all-to-all-start.1 = ((bf16[16,32,336]{2,1,0:T(8,128)(2,1)}), bf16[16,32,336]{2,1,0:T(8,128)(2,1)S(1)}, u32[]{:S(2)}, u32[]{:S(2)}) async-start(bf16[16,32,336]{2,1,0:T(8,128)(2,1)} %get-tuple-element.24), calls=%async_computation.1 | async-start | bytes 786432 | tf_op jit(solution)/shard_map/all_to_all | solution.py:42
  43.2 5.5 %copy-start.6 = (s32[3]{0:T(128)}, s32[3]{0:T(128)S(1)}, u32[]{:S(2)}) copy-start(s32[3]{0:T(128)S(1)} %pad_add_fusion.refs_1_.place_ref) | copy-start | bytes 40
  43.5 0.7 copy-start.12
  44.3 0.7 copy-start.4
  45.0 1.0 copy-start.11
  46.0 0.9 copy-start.13
  48.8 1.5 %collective-permute-start.5 = (bf16[1,4,64,336]{3,2,1,0:T(8,128)(2,1)S(1)}, bf16[1,4,64,336]{3,2,1,0:T(8,128)(2,1)S(1)}, u32[]{:S(2)}, u32[]{:S(2)}) collective-permute-start(bf16[1,4,64,336]{3,2,1,0:T(8,128)(2,1)S(1)} %get-tuple-element.41), channel_id=1, source_target_pairs={{0,16},{16,0},{1,17},{17,1},{2,18},{18,2},{3,19},{19,3},{4,20},{20... | collective-permute-start | bytes 516104 | tf_op jit(solution)/shard_map/ppermute | solution.py:38
  48.9 1.7 %collective-permute-start.8 = (bf16[1,4,64,336]{3,2,1,0:T(8,128)(2,1)S(1)}, bf16[1,4,64,336]{3,2,1,0:T(8,128)(2,1)S(1)}, u32[]{:S(2)}, u32[]{:S(2)}) collective-permute-start(bf16[1,4,64,336]{3,2,1,0:T(8,128)(2,1)S(1)} %get-tuple-element.42), channel_id=1, source_target_pairs={{0,16},{16,0},{1,17},{17,1},{2,18},{18,2},{3,19},{19,3},{4,20},{20... | collective-permute-start | bytes 516104 | tf_op jit(solution)/shard_map/ppermute | solution.py:38
  49.4 1.5 %collective-permute-start.7 = (bf16[1,4,64,336]{3,2,1,0:T(8,128)(2,1)S(1)}, bf16[1,4,64,336]{3,2,1,0:T(8,128)(2,1)S(1)}, u32[]{:S(2)}, u32[]{:S(2)}) collective-permute-start(bf16[1,4,64,336]{3,2,1,0:T(8,128)(2,1)S(1)} %get-tuple-element.43), channel_id=1, source_target_pairs={{0,16},{16,0},{1,17},{17,1},{2,18},{18,2},{3,19},{19,3},{4,20},{20... | collective-permute-start | bytes 516104 | tf_op jit(solution)/shard_map/ppermute | solution.py:38
  49.5 1.7 %collective-permute-start.6 = (bf16[1,4,64,336]{3,2,1,0:T(8,128)(2,1)S(1)}, bf16[1,4,64,336]{3,2,1,0:T(8,128)(2,1)S(1)}, u32[]{:S(2)}, u32[]{:S(2)}) collective-permute-start(bf16[1,4,64,336]{3,2,1,0:T(8,128)(2,1)S(1)} %get-tuple-element.44), channel_id=1, source_target_pairs={{0,16},{16,0},{1,17},{17,1},{2,18},{18,2},{3,19},{19,3},{4,20},{20... | collective-permute-start | bytes 516104 | tf_op jit(solution)/shard_map/ppermute | solution.py:38
  56.5 22.6 %all-to-all-start.2 = ((bf16[16,96,336]{2,1,0:T(8,128)(2,1)}), bf16[16,96,336]{2,1,0:T(8,128)(2,1)S(1)}, u32[]{:S(2)}, u32[]{:S(2)}) async-start(bf16[16,96,336]{2,1,0:T(8,128)(2,1)} %shard_map.87), calls=%async_computation.2 | async-start | bytes 2359296 | tf_op jit(solution)/shard_map/all_to_all | solution.py:42
  100.2 1.2 copy-start
  100.2 7.4 %collective-permute-start.9 = (bf16[16,96,336]{2,1,0:T(8,128)(2,1)S(1)}, bf16[16,96,336]{2,1,0:T(8,128)(2,1)S(1)}, u32[]{:S(2)}, u32[]{:S(2)}) collective-permute-start(bf16[16,96,336]{2,1,0:T(8,128)(2,1)S(1)} %all_to_all.29.own_ref.both_ref), channel_id=1, source_target_pairs={{0,16},{16,0},{1,17},{17,1},{2,18},{18,2},{3,19},{19,3},{4,20},{20... | collective-permute-start | bytes 3096584 | tf_op jit(solution)/shard_map/ppermute | solution.py:38
  101.4 27.7 %all-to-all-start.4 = ((bf16[16,32,336]{2,1,0:T(8,128)(2,1)}), bf16[16,32,336]{2,1,0:T(8,128)(2,1)S(1)}, u32[]{:S(2)}, u32[]{:S(2)}) async-start(bf16[16,32,336]{2,1,0:T(8,128)(2,1)} %shard_map.90), calls=%async_computation.4 | async-start | bytes 786432 | tf_op jit(solution)/shard_map/all_to_all | solution.py:42
  107.5 26.1 %copy-start.1 = (bf16[32,5376]{1,0:T(8,128)(2,1)S(1)}, bf16[32,5376]{1,0:T(8,128)(2,1)}, u32[]{:S(2)}) copy-start(bf16[32,5376]{1,0:T(8,128)(2,1)} %get-tuple-element.36.rows_ref) | copy-start | bytes 1032196
  107.5 26.1 %copy-start.3 = (bf16[1,5376]{1,0:T(2,128)(2,1)S(1)}, bf16[1,5376]{1,0:T(2,128)(2,1)}, u32[]{:S(2)}) copy-start(bf16[1,5376]{1,0:T(2,128)(2,1)} %reshape.20.gain_ref) | copy-start | bytes 32260
  107.5 26.1 %copy-start.5 = (s32[32,128]{1,0:T(8,128)S(1)}, s32[32,128]{1,0:T(8,128)}, u32[]{:S(2)}) copy-start(s32[32,128]{1,0:T(8,128)} %get-tuple-element.25.refs_0_.wanted_ref) | copy-start | bytes 49156
  107.5 1.0 copy-start.17
  114.8 12.2 %collective-permute-start.10 = (bf16[128,512]{1,0:T(8,128)(2,1)}, bf16[128,512]{1,0:T(8,128)(2,1)S(1)}, u32[]{:S(2)}, u32[]{:S(2)}) collective-permute-start(bf16[128,512]{1,0:T(8,128)(2,1)} %get-tuple-element.33), channel_id=1, source_target_pairs={{0,1},{1,2},{2,3},{3,0},{4,5},{5,6},{6,7},{7,4},{8,9},{9,10},{10,1... | collective-permute-start | bytes 393224 | tf_op jit(solution)/shard_map/ppermute | solution.py:34
  117.3 11.9 %collective-permute-start.11 = (bf16[128,512]{1,0:T(8,128)(2,1)}, bf16[128,512]{1,0:T(8,128)(2,1)S(1)}, u32[]{:S(2)}, u32[]{:S(2)}) collective-permute-start(bf16[128,512]{1,0:T(8,128)(2,1)} %get-tuple-element.34), channel_id=1, source_target_pairs={{0,2},{1,3},{2,0},{3,1},{4,6},{5,7},{6,4},{7,5},{8,10},{9,11},{10,... | collective-permute-start | bytes 393224 | tf_op jit(solution)/shard_map/ppermute | solution.py:34
  120.8 12.7 %collective-permute-start.12 = (bf16[128,512]{1,0:T(8,128)(2,1)}, bf16[128,512]{1,0:T(8,128)(2,1)S(1)}, u32[]{:S(2)}, u32[]{:S(2)}) collective-permute-start(bf16[128,512]{1,0:T(8,128)(2,1)} %get-tuple-element.35), channel_id=1, source_target_pairs={{0,3},{1,0},{2,1},{3,2},{4,7},{5,4},{6,5},{7,6},{8,11},{9,8},{10,9... | collective-permute-start | bytes 393224 | tf_op jit(solution)/shard_map/ppermute | solution.py:34
  124.4 15.2 %collective-permute-start.13 = (bf16[336,512]{1,0:T(8,128)(2,1)}, bf16[336,512]{1,0:T(8,128)(2,1)S(1)}, u32[]{:S(2)}, u32[]{:S(2)}) collective-permute-start(bf16[336,512]{1,0:T(8,128)(2,1)} %get-tuple-element.38), channel_id=1, source_target_pairs={{0,4},{4,8},{8,12},{12,0},{1,5},{5,9},{9,13},{13,1},{2,6},{6,10},{... | collective-permute-start | bytes 1032200 | tf_op jit(solution)/shard_map/ppermute | solution.py:34
  125.9 13.8 %collective-permute-start.14 = (bf16[336,512]{1,0:T(8,128)(2,1)}, bf16[336,512]{1,0:T(8,128)(2,1)S(1)}, u32[]{:S(2)}, u32[]{:S(2)}) collective-permute-start(bf16[336,512]{1,0:T(8,128)(2,1)} %get-tuple-element.39), channel_id=1, source_target_pairs={{0,8},{4,12},{8,0},{12,4},{1,9},{5,13},{9,1},{13,5},{2,10},{6,14},... | collective-permute-start | bytes 1032200 | tf_op jit(solution)/shard_map/ppermute | solution.py:34
  127.1 16.1 %collective-permute-start.15 = (bf16[336,512]{1,0:T(8,128)(2,1)}, bf16[336,512]{1,0:T(8,128)(2,1)S(1)}, u32[]{:S(2)}, u32[]{:S(2)}) collective-permute-start(bf16[336,512]{1,0:T(8,128)(2,1)} %get-tuple-element.40), channel_id=1, source_target_pairs={{0,12},{4,0},{8,4},{12,8},{1,13},{5,1},{9,5},{13,9},{2,14},{6,2},{... | collective-permute-start | bytes 1032200 | tf_op jit(solution)/shard_map/ppermute | solution.py:34
  133.6 5.3 %copy-start.15 = (bf16[128,512]{1,0:T(8,128)(2,1)S(1)}, bf16[128,512]{1,0:T(8,128)(2,1)}, u32[]{:S(2)}) copy-start(bf16[128,512]{1,0:T(8,128)(2,1)} %get-tuple-element.32) | copy-start | bytes 393220
  133.6 9.5 %copy-start.14 = (bf16[336,512]{1,0:T(8,128)(2,1)S(1)}, bf16[336,512]{1,0:T(8,128)(2,1)}, u32[]{:S(2)}) copy-start(bf16[336,512]{1,0:T(8,128)(2,1)} %get-tuple-element.37) | copy-start | bytes 1032196

commit v4 on v3

--- a/solution.py
+++ b/solution.py
@@ -42,7 +42,7 @@
     return lax.all_to_all(x, axes, split_axis=0, concat_axis=0, tiled=True)
 
 
-def call(kernel, out_shape, args, flops, scalars=1, scratch=(), after=(), in_hbm=0):
+def call(kernel, out_shape, args, flops, scalars=1, scratch=(), after=(), in_hbm=0, limit=None):
     specs = [pl.BlockSpec(memory_space=pltpu.SMEM)] * scalars
     specs += [pl.BlockSpec(memory_space=pltpu.VMEM)] * (len(args) - scalars - in_hbm)
     specs += [pl.BlockSpec(memory_space=pltpu.HBM)] * in_hbm
@@ -62,7 +62,7 @@
         out_specs=jax.tree.map(lambda _: pl.BlockSpec(memory_space=pltpu.VMEM), out_shape),
         scratch_shapes=scratch,
         compiler_params=pltpu.CompilerParams(
-            vmem_limit_bytes=VMEM_WHOLE if in_hbm else VMEM_LIMIT
+            vmem_limit_bytes=limit or (VMEM_WHOLE if in_hbm else VMEM_LIMIT)
         ),
         cost_estimate=pl.CostEstimate(flops=flops, bytes_accessed=moved, transcendentals=0),
     )(*args)
@@ -90,6 +90,7 @@
     ids = jnp.zeros((n_rows, tok), I32)
     for j in range(N_SEQ):
         ids = jnp.where(which // CAP == j, jnp.broadcast_to(ids_ref[j : j + 1, :], ids.shape), ids)
+    ids = ids % (vocab_rows * N_SECTION * N_SEQ)
     mine = ids // vocab_rows == place_ref[0]
     token = iota((n_rows, tok), 1)
     first = jnp.min(jnp.where(mine, token, tok), axis=1, keepdims=True)
@@ -314,7 +315,8 @@
     shape = jax.ShapeDtypeStruct
 
     ids = vocab_shard[:, 0] * vocab_rows + shard_row
-    all_ids = exchange(jnp.broadcast_to(ids[None], (N_SEQ, tok)), SEQ)
+    vocab = vocab_rows * N_SECTION * N_SEQ
+    all_ids = exchange(ids[None] + vocab * jnp.arange(N_SEQ, dtype=I32)[:, None], SEQ)
 
     ws = [shift(weight, "y", d) for d in range(1, NY)]
     near = swap(cotangent, "z_hi", 1)
@@ -335,6 +337,7 @@
         (shard, all_ids, gain, embed_table),
         flops=2 * N_SEQ * CAP * vocab_rows * model_width,
         in_hbm=1,
+        limit=50 * 1024 * 1024,
         scratch=[
             pltpu.VMEM((N_SEQ, NF * GROUP, feat), F32),
             pltpu.VMEM((6, vocab_rows, model_width // 6), BF16),
@@ -359,18 +362,18 @@
         flops=2 * SLOTS * SLOTS * feat, scalars=0,
     )
     both = exchange(both, SECTION)
-    block_ids = lax.dynamic_slice_in_dim(all_ids, iy * NZH + ix, 1, 0)
+    block_ids = lax.dynamic_slice_in_dim(all_ids, iy * NZH + ix, 1, 0) % vocab
     both = call(
         functools.partial(at_block_kernel, vocab_rows=vocab_rows),
         shape((N_SECTION, width, feat), BF16), (block_ids, both),
         flops=4 * tok * SLOTS * feat, scalars=0,
     )
     both = exchange(both, SECTION)
-    back = call(
+    cut = call(
         to_seq_kernel, shape((N_SEQ, BLOCK_SLOTS, feat), BF16), (both,),
         flops=2 * SLOTS * SLOTS * feat, scalars=0,
     )
-    back = exchange(back, SEQ)
+    back = exchange(cut, SEQ)
 
     products = call(
         products_kernel,
@@ -378,6 +381,7 @@
         (where, both, swap(both, "core", 1), *cots, *ws),
         flops=4 * NB * tok * NF * feat * cols,
         in_hbm=2 + NY,
+        after=(cut,),
         scratch=[
             pltpu.VMEM((NZH, tok, cols), BF16),
             pltpu.VMEM((NY, feat, cols), BF16),
@@ -390,7 +394,7 @@
     weight_grad = sum_f32([grad[0], *grad_parts]).astype(BF16)
     projected = sum_f32([proj[0], *proj_parts]).astype(BF16)
 
-    table_grad = table_call(back, rows, gain, wanted, vocab_rows, after=proj_parts)
+    table_grad = table_call(back, rows, gain, wanted, vocab_rows, after=proj_parts[:1])
     return projected, table_grad, weight_grad
 
 

time: 145 us -> 145 us (level)
    unnamed x36 -> x28, local copies, waits for them, and re-layouts: 4.43 us -> 5.44 us
  transfers between devices with their start and end apart: 20 -> 20, of which waited for: 10 -> 11; matrix products, arithmetic and copies ran while one was open for 3% -> 2% of each run, Pallas kernels for 14% -> 13%
where the time goes in v4:
time: 145 us; the launch traced here: 144 us
  starting transfers between devices  52.8 us (36%)
  waiting for transfers between devices  38.4 us (26%)
  Pallas kernels  21.1 us (15%)
  blocking collectives  20.6 us (14%)
  local copies, waits for them, and re-layouts  6.25 us (4%)
  other arithmetic  4.32 us (3%)
    all_to_all x4, starting transfers between devices, exchange(): return lax.all_to_all(x, axes, split_axis=0, concat_axis=0, tiled=True)  28.4 us
    all_to_all x4, waiting for transfers between devices, exchange(): return lax.all_to_all(x, axes, split_axis=0, concat_axis=0, tiled=True)  28 us
    all_to_all x1, blocking collectives, exchange(): return lax.all_to_all(x, axes, split_axis=0, concat_axis=0, tiled=True)  20.6 us
    ppermute x9, starting transfers between devices, shift(): return lax.ppermute(x, axis, [(i, (i + by) % size) for i in range(size)])  19.3 us
    pallas_call x6, Pallas kernels, call(): pl.pallas_call(kernel, out_shape=out_shape, in_specs=specs, out_specs=jax...  15.8 us
    ppermute x9, waiting for transfers between devices, shift(): return lax.ppermute(x, axis, [(i, (i + by) % size) for i in range(size)])  8.03 us
    unnamed x28, local copies, waits for them, and re-layouts  5.44 us
    pallas_call x1, Pallas kernels, table_call(): pl.pallas_call(table_kernel, grid=(steps,), out_shape=jax.ShapeDtypeStruc...  5.28 us
  transfers between devices with their start and end apart: 20, of which 11 were waited for; matrix products, arithmetic and copies ran while one was open for 2% of the time, Pallas kernels for 13%

profile of v4, /device:TPU:8, one launch (start us, length us, event | category | flops | bytes accessed | tf_op | source)
XLA Modules:
  0.0 144.3 jit_solution(6643535747883637743)
XLA Ops:
  0.6 2.3 %collective-permute-start.3 = (bf16[336,512]{1,0:T(8,128)(2,1)}, bf16[336,512]{1,0:T(8,128)(2,1)S(1)}, u32[]{:S(2)}, u32[]{:S(2)}) collective-permute-start(bf16[336,512]{1,0:T(8,128)(2,1)} %refs_6_.1), channel_id=1, source_target_pairs={{0,12},{4,0},{8,4},{12,8},{1,13},{5,1},{9,5},{13,9},{2,14},{6,2},{... | collective-permute-start | bytes 1032200 | tf_op jit(solution)/shard_map/ppermute | solution.py:34
  2.9 0.9 collective-permute-start.2
  3.7 1.9 %collective-permute-start.1 = (bf16[336,512]{1,0:T(8,128)(2,1)}, bf16[336,512]{1,0:T(8,128)(2,1)S(1)}, u32[]{:S(2)}, u32[]{:S(2)}) collective-permute-start(bf16[336,512]{1,0:T(8,128)(2,1)} %refs_6_.1), channel_id=1, source_target_pairs={{0,4},{4,8},{8,12},{12,0},{1,5},{5,9},{9,13},{13,1},{2,6},{6,10},{... | collective-permute-start | bytes 1032200 | tf_op jit(solution)/shard_map/ppermute | solution.py:34
  5.6 3.3 %collective-permute-start = (bf16[128,512]{1,0:T(8,128)(2,1)}, bf16[128,512]{1,0:T(8,128)(2,1)S(1)}, u32[]{:S(2)}, u32[]{:S(2)}) collective-permute-start(bf16[128,512]{1,0:T(8,128)(2,1)} %param.11), channel_id=1, source_target_pairs={{0,1},{1,0},{2,3},{3,2},{4,5},{5,4},{6,7},{7,6},{8,9},{9,8},{10,11... | collective-permute-start | bytes 393224 | tf_op jit(solution)/shard_map/ppermute | solution.py:38
  8.9 0.7 bitcast_add_fusion
  9.6 0.7 broadcast_add_fusion
  10.3 8.5 %all-to-all-start = ((s32[16,1,128]{2,1,0:T(1,128)}), s32[16,1,128]{2,1,0:T(1,128)S(1)}, u32[]{:S(2)}, u32[]{:S(2)}) async-start(s32[16,1,128]{2,1,0:T(1,128)} %broadcast_add_fusion), calls=%async_computation | async-start | bytes 16384 | tf_op jit(solution)/shard_map/all_to_all | solution.py:42
  18.8 0.7 reshape.60.gain_ref
  19.5 7.8 %all-to-all-done = s32[16,1,128]{2,1,0:T(1,128)S(1)} async-done(((s32[16,1,128]{2,1,0:T(1,128)}), s32[16,1,128]{2,1,0:T(1,128)S(1)}, u32[]{:S(2)}, u32[]{:S(2)}) %all-to-all-start) | async-done | bytes 8224 | tf_op jit(solution)/shard_map/all_to_all | solution.py:42
  27.3 0.8 copy-done.5
  28.1 1.0 pad_maximum_fusion.1.refs_2_.refs_4_
  29.2 0.7 collective-permute-start.4
  29.9 4.6 %shard_map.85 = (bf16[16,32,336]{2,1,0:T(8,128)(2,1)}, bf16[32,5376]{1,0:T(8,128)(2,1)S(1)}, s32[32,128]{1,0:T(8,128)S(1)}) custom-call(s32[1]{0:T(128)} %bitcast.2.place_ref, s32[16,128]{1,0:T(8,128)S(1)} %bitcast.9, bf16[1,5376]{1,0:T(2,128)(2,1)S(1)} %reshape.60.gain_ref, bf16[512,5376]{1,0:T(8,128)(2,1)} %table_ref.1), custom_call_target="tpu_custom_call" | custom-call | flops 176160768 | bytes 6228484 | tf_op jit(solution)/shard_map/pallas_call | solution.py:58
  34.4 8.7 %all-to-all-start.1 = ((bf16[16,32,336]{2,1,0:T(8,128)(2,1)}), bf16[16,32,336]{2,1,0:T(8,128)(2,1)S(1)}, u32[]{:S(2)}, u32[]{:S(2)}) async-start(bf16[16,32,336]{2,1,0:T(8,128)(2,1)} %get-tuple-element.24), calls=%async_computation.1 | async-start | bytes 786432 | tf_op jit(solution)/shard_map/all_to_all | solution.py:42
  43.2 1.2 collective-permute-done.4.refs_3_.refs_5_
  44.4 0.7 copy-done.9
  45.1 1.0 copy-done.6
  46.1 1.0 copy-done.8
  47.1 0.9 copy-done.10
  48.0 1.8 %shard_map.86 = (f32[4,4,64,336]{3,2,1,0:T(8,128)S(1)}, bf16[4,4,64,336]{3,2,1,0:T(8,128)(2,1)S(1)}) custom-call(s32[32,128]{1,0:T(8,128)S(1)} %get-tuple-element.25.refs_0_.wanted_ref, s32[3]{0:T(128)S(1)} %pad_add_fusion.refs_1_, bf16[2,128,512]{2,1,0:T(8,128)(2,1)S(1)} %pad_maximum_fusion.1.refs_2_.refs_4_, bf16[2,128,512]{2,1,0:T(8,128)(2,1)S(1)} %copy-done.10, ...), custom_call_target="tpu_custom_call" | custom-call | flops 704643072 | bytes 3964940 | tf_op jit(solution)/shard_map/pallas_call | solution.py:58
  50.1 0.5 collective-permute-start.8
  50.6 0.4 collective-permute-start.6
  51.1 0.4 collective-permute-done.5
  51.5 0.3 collective-permute-done.8
  51.8 0.3 collective-permute-done.7
  52.0 0.3 collective-permute-done.6
  52.5 2.1 %all-to-all-done.1.got_ref = bf16[16,32,336]{2,1,0:T(8,128)(2,1)S(1)} async-done(((bf16[16,32,336]{2,1,0:T(8,128)(2,1)}), bf16[16,32,336]{2,1,0:T(8,128)(2,1)S(1)}, u32[]{:S(2)}, u32[]{:S(2)}) %all-to-all-start.1) | async-done | bytes 344096 | tf_op jit(solution)/shard_map/all_to_all | solution.py:42
  54.6 1.5 %shard_map.87 = bf16[16,96,336]{2,1,0:T(8,128)(2,1)} custom-call(bf16[16,32,336]{2,1,0:T(8,128)(2,1)S(1)} %all-to-all-done.1.got_ref, f32[4,4,64,336]{3,2,1,0:T(8,128)S(1)} %get-tuple-element.30.keep_ref, bf16[4,4,64,336]{3,2,1,0:T(8,128)(2,1)S(1)} %pad_maximum_fusion.recv_ref), custom_call_target="tpu_custom_call" | custom-call | flops 176160768 | bytes 3440640 | tf_op jit(solution)/shard_map/pallas_call | solution.py:58
  56.2 4.6 %all-to-all-start.2 = ((bf16[16,96,336]{2,1,0:T(8,128)(2,1)}), bf16[16,96,336]{2,1,0:T(8,128)(2,1)S(1)}, u32[]{:S(2)}, u32[]{:S(2)}) async-start(bf16[16,96,336]{2,1,0:T(8,128)(2,1)} %shard_map.87), calls=%async_computation.2 | async-start | bytes 2359296 | tf_op jit(solution)/shard_map/all_to_all | solution.py:42
  60.8 18.0 %all-to-all-done.2.both_ref = bf16[16,96,336]{2,1,0:T(8,128)(2,1)S(1)} async-done(((bf16[16,96,336]{2,1,0:T(8,128)(2,1)}), bf16[16,96,336]{2,1,0:T(8,128)(2,1)S(1)}, u32[]{:S(2)}, u32[]{:S(2)}) %all-to-all-start.2) | async-done | bytes 1032224 | tf_op jit(solution)/shard_map/all_to_all | solution.py:42
  78.9 0.5 shard_map.88
  79.4 20.6 %all_to_all.29.both_ref.refs_2_ = bf16[16,96,336]{2,1,0:T(8,128)(2,1)S(1)} all-to-all(bf16[16,96,336]{2,1,0:T(8,128)(2,1)S(1)} %shard_map.88), channel_id=1, replica_groups=mesh['x'=4,'z_lo'=2,'core'=2,'y'=4,'z_hi'=4] {'x','z_lo','core'}, dimensions={0} | all-to-all | bytes 2064384 | tf_op jit(solution)/shard_map/all_to_all | solution.py:42
  100.0 1.2 shard_map.89.refs_0_
  101.2 6.6 %all-to-all-start.4 = ((bf16[16,32,336]{2,1,0:T(8,128)(2,1)}), bf16[16,32,336]{2,1,0:T(8,128)(2,1)S(1)}, u32[]{:S(2)}, u32[]{:S(2)}) async-start(bf16[16,32,336]{2,1,0:T(8,128)(2,1)} %shard_map.89.refs_0_), calls=%async_computation.4 | async-start | bytes 786432 | tf_op jit(solution)/shard_map/all_to_all | solution.py:42
  107.8 1.0 copy-done.13
  108.8 6.2 %shard_map.90 = (bf16[128,512]{1,0:T(8,128)(2,1)}, bf16[128,512]{1,0:T(8,128)(2,1)}, bf16[128,512]{1,0:T(8,128)(2,1)}, bf16[128,512]{1,0:T(8,128)(2,1)}, bf16[33...) custom-call(bf16[16,32,336]{2,1,0:T(8,128)(2,1)} %shard_map.89.refs_0_, ...), custom_call_target="tpu_custom_call" | custom-call | flops 1409286144 | bytes 5865484 | tf_op jit(solution)/shard_map/pallas_call | solution.py:58
  115.0 2.4 %collective-permute-start.10 = (bf16[128,512]{1,0:T(8,128)(2,1)}, bf16[128,512]{1,0:T(8,128)(2,1)S(1)}, u32[]{:S(2)}, u32[]{:S(2)}) collective-permute-start(bf16[128,512]{1,0:T(8,128)(2,1)} %get-tuple-element.33), channel_id=1, source_target_pairs={{0,1},{1,2},{2,3},{3,0},{4,5},{5,6},{6,7},{7,4},{8,9},{9,10},{10,1... | collective-permute-start | bytes 393224 | tf_op jit(solution)/shard_map/ppermute | solution.py:34
  117.5 3.6 %collective-permute-start.11 = (bf16[128,512]{1,0:T(8,128)(2,1)}, bf16[128,512]{1,0:T(8,128)(2,1)S(1)}, u32[]{:S(2)}, u32[]{:S(2)}) collective-permute-start(bf16[128,512]{1,0:T(8,128)(2,1)} %get-tuple-element.34), channel_id=1, source_target_pairs={{0,2},{1,3},{2,0},{3,1},{4,6},{5,7},{6,4},{7,5},{8,10},{9,11},{10,... | collective-permute-start | bytes 393224 | tf_op jit(solution)/shard_map/ppermute | solution.py:34
  121.0 3.6 %collective-permute-start.12 = (bf16[128,512]{1,0:T(8,128)(2,1)}, bf16[128,512]{1,0:T(8,128)(2,1)S(1)}, u32[]{:S(2)}, u32[]{:S(2)}) collective-permute-start(bf16[128,512]{1,0:T(8,128)(2,1)} %get-tuple-element.35), channel_id=1, source_target_pairs={{0,3},{1,0},{2,1},{3,2},{4,7},{5,4},{6,5},{7,6},{8,11},{9,8},{10,9... | collective-permute-start | bytes 393224 | tf_op jit(solution)/shard_map/ppermute | solution.py:34
  124.6 1.5 %collective-permute-start.13 = (bf16[336,512]{1,0:T(8,128)(2,1)}, bf16[336,512]{1,0:T(8,128)(2,1)S(1)}, u32[]{:S(2)}, u32[]{:S(2)}) collective-permute-start(bf16[336,512]{1,0:T(8,128)(2,1)} %get-tuple-element.38), channel_id=1, source_target_pairs={{0,4},{4,8},{8,12},{12,0},{1,5},{5,9},{9,13},{13,1},{2,6},{6,10},{... | collective-permute-start | bytes 1032200 | tf_op jit(solution)/shard_map/ppermute | solution.py:34
  126.1 1.2 collective-permute-start.14
  127.3 2.0 %collective-permute-start.15 = (bf16[336,512]{1,0:T(8,128)(2,1)}, bf16[336,512]{1,0:T(8,128)(2,1)S(1)}, u32[]{:S(2)}, u32[]{:S(2)}) collective-permute-start(bf16[336,512]{1,0:T(8,128)(2,1)} %get-tuple-element.40), channel_id=1, source_target_pairs={{0,12},{4,0},{8,4},{12,8},{1,13},{5,1},{9,5},{13,9},{2,14},{6,2},{... | collective-permute-start | bytes 1032200 | tf_op jit(solution)/shard_map/ppermute | solution.py:34
  129.3 5.3 %shard_map.91 = bf16[512,5376]{1,0:T(8,128)(2,1)} custom-call(bf16[16,32,336]{2,1,0:T(8,128)(2,1)S(1)} %all-to-all-done.4.back_ref, bf16[32,5376]{1,0:T(8,128)(2,1)S(1)} %get-tuple-element.36.rows_ref, bf16[1,5376]{1,0:T(2,128)(2,1)S(1)} %reshape.60.gain_ref, s32[32,128]{1,0:T(8,128)S(1)} %get-tuple-element.25.refs_0_.wanted_ref, ...), custom_call_target="tpu_custom_call" | custom-call | flops 176160768 | bytes 5505024 | tf_op jit(solution)/shard_map/pallas_call | solution.py:280
  134.6 0.7 add_convert_fusion.1
  135.3 0.5 collective-permute-done.13
  135.8 3.0 %collective-permute-done.14 = bf16[336,512]{1,0:T(8,128)(2,1)S(1)} collective-permute-done((bf16[336,512]{1,0:T(8,128)(2,1)}, bf16[336,512]{1,0:T(8,128)(2,1)S(1)}, u32[]{:S(2)}, u32[]{:S(2)}) %collective-permute-start.14) | collective-permute-done | bytes 344096 | tf_op jit(solution)/shard_map/ppermute | solution.py:34
  138.8 4.5 %collective-permute-done.15 = bf16[336,512]{1,0:T(8,128)(2,1)S(1)} collective-permute-done((bf16[336,512]{1,0:T(8,128)(2,1)}, bf16[336,512]{1,0:T(8,128)(2,1)S(1)}, u32[]{:S(2)}, u32[]{:S(2)}) %collective-permute-start.15) | collective-permute-done | bytes 344096 | tf_op jit(solution)/shard_map/ppermute | solution.py:34
  143.4 0.9 add_convert_fusion
  (39 shorter events, 0.6 us)
Async XLA Ops:
  0.6 26.7 %collective-permute-start.3 = (bf16[336,512]{1,0:T(8,128)(2,1)}, bf16[336,512]{1,0:T(8,128)(2,1)S(1)}, u32[]{:S(2)}, u32[]{:S(2)}) collective-permute-start(bf16[336,512]{1,0:T(8,128)(2,1)} %refs_6_.1), channel_id=1, source_target_pairs={{0,12},{4,0},{8,4},{12,8},{1,13},{5,1},{9,5},{13,9},{2,14},{6,2},{... | collective-permute-start | bytes 1032200 | tf_op jit(solution)/shard_map/ppermute | solution.py:34
  2.9 24.4 %collective-permute-start.2 = (bf16[336,512]{1,0:T(8,128)(2,1)}, bf16[336,512]{1,0:T(8,128)(2,1)S(1)}, u32[]{:S(2)}, u32[]{:S(2)}) collective-permute-start(bf16[336,512]{1,0:T(8,128)(2,1)} %refs_6_.1), channel_id=1, source_target_pairs={{0,8},{4,12},{8,0},{12,4},{1,9},{5,13},{9,1},{13,5},{2,10},{6,14},... | collective-permute-start | bytes 1032200 | tf_op jit(solution)/shard_map/ppermute | solution.py:34
  3.7 24.4 %collective-permute-start.1 = (bf16[336,512]{1,0:T(8,128)(2,1)}, bf16[336,512]{1,0:T(8,128)(2,1)S(1)}, u32[]{:S(2)}, u32[]{:S(2)}) collective-permute-start(bf16[336,512]{1,0:T(8,128)(2,1)} %refs_6_.1), channel_id=1, source_target_pairs={{0,4},{4,8},{8,12},{12,0},{1,5},{5,9},{9,13},{13,1},{2,6},{6,10},{... | collective-permute-start | bytes 1032200 | tf_op jit(solution)/shard_map/ppermute | solution.py:34
  5.6 21.7 %collective-permute-start = (bf16[128,512]{1,0:T(8,128)(2,1)}, bf16[128,512]{1,0:T(8,128)(2,1)S(1)}, u32[]{:S(2)}, u32[]{:S(2)}) collective-permute-start(bf16[128,512]{1,0:T(8,128)(2,1)} %param.11), channel_id=1, source_target_pairs={{0,1},{1,0},{2,3},{3,2},{4,5},{5,4},{6,7},{7,6},{8,9},{9,8},{10,11... | collective-permute-start | bytes 393224 | tf_op jit(solution)/shard_map/ppermute | solution.py:38
  10.3 17.0 %all-to-all-start = ((s32[16,1,128]{2,1,0:T(1,128)}), s32[16,1,128]{2,1,0:T(1,128)S(1)}, u32[]{:S(2)}, u32[]{:S(2)}) async-start(s32[16,1,128]{2,1,0:T(1,128)} %broadcast_add_fusion), calls=%async_computation | async-start | bytes 16384 | tf_op jit(solution)/shard_map/all_to_all | solution.py:42
  27.3 17.8 %copy-start.4 = (bf16[336,512]{1,0:T(8,128)(2,1)}, bf16[336,512]{1,0:T(8,128)(2,1)S(1)}, u32[]{:S(2)}) copy-start(bf16[336,512]{1,0:T(8,128)(2,1)S(1)} %collective-permute-done.3.refs_7_.refs_9_) | copy-start | bytes 1032196
  27.3 0.8 copy-start.5
  28.1 6.3 %copy-start.7 = (bf16[336,512]{1,0:T(8,128)(2,1)}, bf16[336,512]{1,0:T(8,128)(2,1)S(1)}, u32[]{:S(2)}) copy-start(bf16[336,512]{1,0:T(8,128)(2,1)S(1)} %collective-permute-done.1.refs_5_.refs_7_) | copy-start | bytes 1032196
  29.2 16.0 %copy-start.1 = (bf16[2,128,512]{2,1,0:T(8,128)(2,1)}, bf16[2,128,512]{2,1,0:T(8,128)(2,1)S(1)}, u32[]{:S(2)}) copy-start(bf16[2,128,512]{2,1,0:T(8,128)(2,1)S(1)} %pad_maximum_fusion.1.refs_2_.refs_4_) | copy-start | bytes 786436
  29.2 15.2 %collective-permute-start.4 = (bf16[2,128,512]{2,1,0:T(8,128)(2,1)S(1)}, bf16[2,128,512]{2,1,0:T(8,128)(2,1)S(1)}, u32[]{:S(2)}, u32[]{:S(2)}) collective-permute-start(bf16[2,128,512]{2,1,0:T(8,128)(2,1)S(1)} %pad_maximum_fusion.1.refs_2_.refs_4_), channel_id=1, source_target_pairs={{0,2},{1,3},{2,0},{3,1},{4,6},{5,7},{6,4},{7,5},{8,10},{9,11},{10,... | collective-permute-start | bytes 786440 | tf_op jit(solution)/shard_map/ppermute | solution.py:38
  29.9 15.3 %copy-start.3 = (bf16[336,512]{1,0:T(8,128)(2,1)S(1)}, bf16[336,512]{1,0:T(8,128)(2,1)}, u32[]{:S(2)}) copy-start(bf16[336,512]{1,0:T(8,128)(2,1)} %refs_6_.1) | copy-start | bytes 1032196
  34.4 20.2 %all-to-all-start.1 = ((bf16[16,32,336]{2,1,0:T(8,128)(2,1)}), bf16[16,32,336]{2,1,0:T(8,128)(2,1)S(1)}, u32[]{:S(2)}, u32[]{:S(2)}) async-start(bf16[16,32,336]{2,1,0:T(8,128)(2,1)} %get-tuple-element.24), calls=%async_computation.1 | async-start | bytes 786432 | tf_op jit(solution)/shard_map/all_to_all | solution.py:42
  43.2 6.6 %copy-start.2 = (s32[3]{0:T(128)}, s32[3]{0:T(128)S(1)}, u32[]{:S(2)}) copy-start(s32[3]{0:T(128)S(1)} %pad_add_fusion.refs_1_) | copy-start | bytes 40
  44.4 0.7 copy-start.9
  45.1 1.0 copy-start.6
  46.1 1.0 copy-start.8
  47.1 0.9 copy-start.10
  50.0 1.5 %collective-permute-start.5 = (bf16[1,4,64,336]{3,2,1,0:T(8,128)(2,1)S(1)}, bf16[1,4,64,336]{3,2,1,0:T(8,128)(2,1)S(1)}, u32[]{:S(2)}, u32[]{:S(2)}) collective-permute-start(bf16[1,4,64,336]{3,2,1,0:T(8,128)(2,1)S(1)} %get-tuple-element.41), channel_id=1, source_target_pairs={{0,16},{16,0},{1,17},{17,1},{2,18},{18,2},{3,19},{19,3},{4,20},{20... | collective-permute-start | bytes 516104 | tf_op jit(solution)/shard_map/ppermute | solution.py:38
  50.1 1.7 %collective-permute-start.8 = (bf16[1,4,64,336]{3,2,1,0:T(8,128)(2,1)S(1)}, bf16[1,4,64,336]{3,2,1,0:T(8,128)(2,1)S(1)}, u32[]{:S(2)}, u32[]{:S(2)}) collective-permute-start(bf16[1,4,64,336]{3,2,1,0:T(8,128)(2,1)S(1)} %get-tuple-element.42), channel_id=1, source_target_pairs={{0,16},{16,0},{1,17},{17,1},{2,18},{18,2},{3,19},{19,3},{4,20},{20... | collective-permute-start | bytes 516104 | tf_op jit(solution)/shard_map/ppermute | solution.py:38
  50.5 1.5 %collective-permute-start.7 = (bf16[1,4,64,336]{3,2,1,0:T(8,128)(2,1)S(1)}, bf16[1,4,64,336]{3,2,1,0:T(8,128)(2,1)S(1)}, u32[]{:S(2)}, u32[]{:S(2)}) collective-permute-start(bf16[1,4,64,336]{3,2,1,0:T(8,128)(2,1)S(1)} %get-tuple-element.43), channel_id=1, source_target_pairs={{0,16},{16,0},{1,17},{17,1},{2,18},{18,2},{3,19},{19,3},{4,20},{20... | collective-permute-start | bytes 516104 | tf_op jit(solution)/shard_map/ppermute | solution.py:38
  50.6 1.7 %collective-permute-start.6 = (bf16[1,4,64,336]{3,2,1,0:T(8,128)(2,1)S(1)}, bf16[1,4,64,336]{3,2,1,0:T(8,128)(2,1)S(1)}, u32[]{:S(2)}, u32[]{:S(2)}) collective-permute-start(bf16[1,4,64,336]{3,2,1,0:T(8,128)(2,1)S(1)} %get-tuple-element.44), channel_id=1, source_target_pairs={{0,16},{16,0},{1,17},{17,1},{2,18},{18,2},{3,19},{19,3},{4,20},{20... | collective-permute-start | bytes 516104 | tf_op jit(solution)/shard_map/ppermute | solution.py:38
  56.2 22.7 %all-to-all-start.2 = ((bf16[16,96,336]{2,1,0:T(8,128)(2,1)}), bf16[16,96,336]{2,1,0:T(8,128)(2,1)S(1)}, u32[]{:S(2)}, u32[]{:S(2)}) async-start(bf16[16,96,336]{2,1,0:T(8,128)(2,1)} %shard_map.87), calls=%async_computation.2 | async-start | bytes 2359296 | tf_op jit(solution)/shard_map/all_to_all | solution.py:42
  100.0 1.2 copy-start
  100.0 7.8 %collective-permute-start.9 = (bf16[16,96,336]{2,1,0:T(8,128)(2,1)S(1)}, bf16[16,96,336]{2,1,0:T(8,128)(2,1)S(1)}, u32[]{:S(2)}, u32[]{:S(2)}) collective-permute-start(bf16[16,96,336]{2,1,0:T(8,128)(2,1)S(1)} %all_to_all.29.both_ref.refs_2_), channel_id=1, source_target_pairs={{0,16},{16,0},{1,17},{17,1},{2,18},{18,2},{3,19},{19,3},{4,20},{20... | collective-permute-start | bytes 3096584 | tf_op jit(solution)/shard_map/ppermute | solution.py:38
  101.2 28.2 %all-to-all-start.4 = ((bf16[16,32,336]{2,1,0:T(8,128)(2,1)}), bf16[16,32,336]{2,1,0:T(8,128)(2,1)S(1)}, u32[]{:S(2)}, u32[]{:S(2)}) async-start(bf16[16,32,336]{2,1,0:T(8,128)(2,1)} %shard_map.89.refs_0_), calls=%async_computation.4 | async-start | bytes 786432 | tf_op jit(solution)/shard_map/all_to_all | solution.py:42
  107.8 1.0 copy-start.13
  115.0 12.2 %collective-permute-start.10 = (bf16[128,512]{1,0:T(8,128)(2,1)}, bf16[128,512]{1,0:T(8,128)(2,1)S(1)}, u32[]{:S(2)}, u32[]{:S(2)}) collective-permute-start(bf16[128,512]{1,0:T(8,128)(2,1)} %get-tuple-element.33), channel_id=1, source_target_pairs={{0,1},{1,2},{2,3},{3,0},{4,5},{5,6},{6,7},{7,4},{8,9},{9,10},{10,1... | collective-permute-start | bytes 393224 | tf_op jit(solution)/shard_map/ppermute | solution.py:34
  117.5 17.1 %collective-permute-start.11 = (bf16[128,512]{1,0:T(8,128)(2,1)}, bf16[128,512]{1,0:T(8,128)(2,1)S(1)}, u32[]{:S(2)}, u32[]{:S(2)}) collective-permute-start(bf16[128,512]{1,0:T(8,128)(2,1)} %get-tuple-element.34), channel_id=1, source_target_pairs={{0,2},{1,3},{2,0},{3,1},{4,6},{5,7},{6,4},{7,5},{8,10},{9,11},{10,... | collective-permute-start | bytes 393224 | tf_op jit(solution)/shard_map/ppermute | solution.py:34
  121.0 13.6 %collective-permute-start.12 = (bf16[128,512]{1,0:T(8,128)(2,1)}, bf16[128,512]{1,0:T(8,128)(2,1)S(1)}, u32[]{:S(2)}, u32[]{:S(2)}) collective-permute-start(bf16[128,512]{1,0:T(8,128)(2,1)} %get-tuple-element.35), channel_id=1, source_target_pairs={{0,3},{1,0},{2,1},{3,2},{4,7},{5,4},{6,5},{7,6},{8,11},{9,8},{10,9... | collective-permute-start | bytes 393224 | tf_op jit(solution)/shard_map/ppermute | solution.py:34
  124.6 11.2 %collective-permute-start.13 = (bf16[336,512]{1,0:T(8,128)(2,1)}, bf16[336,512]{1,0:T(8,128)(2,1)S(1)}, u32[]{:S(2)}, u32[]{:S(2)}) collective-permute-start(bf16[336,512]{1,0:T(8,128)(2,1)} %get-tuple-element.38), channel_id=1, source_target_pairs={{0,4},{4,8},{8,12},{12,0},{1,5},{5,9},{9,13},{13,1},{2,6},{6,10},{... | collective-permute-start | bytes 1032200 | tf_op jit(solution)/shard_map/ppermute | solution.py:34
  126.1 12.7 %collective-permute-start.14 = (bf16[336,512]{1,0:T(8,128)(2,1)}, bf16[336,512]{1,0:T(8,128)(2,1)S(1)}, u32[]{:S(2)}, u32[]{:S(2)}) collective-permute-start(bf16[336,512]{1,0:T(8,128)(2,1)} %get-tuple-element.39), channel_id=1, source_target_pairs={{0,8},{4,12},{8,0},{12,4},{1,9},{5,13},{9,1},{13,5},{2,10},{6,14},... | collective-permute-start | bytes 1032200 | tf_op jit(solution)/shard_map/ppermute | solution.py:34
  127.3 16.1 %collective-permute-start.15 = (bf16[336,512]{1,0:T(8,128)(2,1)}, bf16[336,512]{1,0:T(8,128)(2,1)S(1)}, u32[]{:S(2)}, u32[]{:S(2)}) collective-permute-start(bf16[336,512]{1,0:T(8,128)(2,1)} %get-tuple-element.40), channel_id=1, source_target_pairs={{0,12},{4,0},{8,4},{12,8},{1,13},{5,1},{9,5},{13,9},{2,14},{6,2},{... | collective-permute-start | bytes 1032200 | tf_op jit(solution)/shard_map/ppermute | solution.py:34
  129.3 5.3 %copy-start.12 = (bf16[128,512]{1,0:T(8,128)(2,1)S(1)}, bf16[128,512]{1,0:T(8,128)(2,1)}, u32[]{:S(2)}) copy-start(bf16[128,512]{1,0:T(8,128)(2,1)} %get-tuple-element.32) | copy-start | bytes 393220
  129.3 14.0 %copy-start.11 = (bf16[336,512]{1,0:T(8,128)(2,1)S(1)}, bf16[336,512]{1,0:T(8,128)(2,1)}, u32[]{:S(2)}) copy-start(bf16[336,512]{1,0:T(8,128)(2,1)} %get-tuple-element.37) | copy-start | bytes 1032196
